TPU v7x, 32 devices: a whole 2x2x4 slice. The times are simulated.
32 devices in a mesh: row: 4 (over y, core), col: 8 (over z, x).
Axes of the slice: x: 2, y: 2, z: 4, core: 2. Of those that a mesh axis runs over, the one named last changes fastest.
Arguments:
- wavefunction: bfloat16 [4096, 4096], P('row', 'col'), may hold values from -6 to 6
- left_env: bfloat16 [4, 4096, 4096], P(None, 'row'), may hold values from -0.09375 to 0.09375
- right_env: bfloat16 [4, 4096, 4096], P(None, None, 'col'), may hold values from -0.09375 to 0.09375
- filled_blocks: int32 [32, 32], replicated, may hold values 0 or 1
- term_columns: int32 [4, 32], replicated, may hold values 0 or 1
Outputs:
- product: bfloat16 [4096, 4096], P('row', 'col')
All inputs are finite; a program needn't handle non-finite values.
Results may differ from a plain program's by a relative error of at most 0.001.
Values may be sent and summed in bfloat16 or wider, within the bound.
No kernel may reach another device: no remote copies, remote signals or barrier semaphores. Data moves between devices by JAX's collectives and lax.ppermute only.
A program may use at most 128 MiB of HBM per device.

v0:
```python
import functools

import jax
import jax.numpy as jnp
from jax import lax
from jax.experimental import pallas as pl
from jax.experimental.pallas import tpu as pltpu
from jax.sharding import PartitionSpec as P

BLOCK = 128
CORES = 2
ITEMS = 2
GROUP = 8
SIDE = 4
CHUNK = 8
AXES = ("row", "col")
VMEM_LIMIT = 58 * 1024 * 1024


class Places:
    def __init__(self, row_devices, col_devices):
        self.rows, self.cols = row_devices, col_devices
        self.y = row_devices // CORES
        self.x = 1
        while self.x * self.x * 4 <= col_devices and col_devices % (self.x * 2) == 0:
            self.x *= 2
        self.z = col_devices // self.x

    def flat(self, y, core, z, x):
        return (y * CORES + core) * self.cols + z * self.x + x

    def shift(self, dy=0, dz=0, dx=0, dcore=0):
        perm = []
        for y in range(self.y):
            for core in range(CORES):
                for z in range(self.z):
                    for x in range(self.x):
                        there = self.flat(
                            (y + dy) % self.y, (core + dcore) % CORES, (z + dz) % self.z, (x + dx) % self.x
                        )
                        perm.append((self.flat(y, core, z, x), there))
        return perm


def compress_kernel(ranges, row_blocks, col_blocks, filled, psi, *rest):
    outs, sems = rest[: len(ranges)], rest[len(ranges)]
    row0 = lax.axis_index("row") * row_blocks
    col0 = lax.axis_index("col") * col_blocks

    def copy(i, slot, kb, cb):
        return pltpu.make_async_copy(
            psi.at[pl.ds(kb * BLOCK, BLOCK), pl.ds(cb * BLOCK, BLOCK)], outs[i].at[slot - ranges[i][0]], sems.at[i, slot]
        )

    count = jnp.int32(0)
    for kb in range(row_blocks):
        for cb in range(col_blocks):
            here = filled[row0 + kb, col0 + cb]
            for i, (low, high) in enumerate(ranges):
                @pl.when((here != 0) & (count >= low) & (count < high))
                def _():
                    copy(i, count, kb, cb).start()
            count = count + here
    for i, (low, high) in enumerate(ranges):
        for slot in range(low, high):
            @pl.when(slot < count)
            def _():
                copy(i, slot, 0, 0).wait()


def compress(psi, filled, ranges):
    row_blocks, col_blocks = psi.shape[0] // BLOCK, psi.shape[1] // BLOCK
    return pl.pallas_call(
        functools.partial(compress_kernel, ranges, row_blocks, col_blocks),
        out_shape=[jax.ShapeDtypeStruct((high - low, BLOCK, BLOCK), psi.dtype) for low, high in ranges],
        in_specs=[pl.BlockSpec(memory_space=pltpu.SMEM), pl.BlockSpec(memory_space=pltpu.VMEM)],
        out_specs=[pl.BlockSpec(memory_space=pltpu.VMEM)] * len(ranges),
        scratch_shapes=[pltpu.SemaphoreType.DMA((len(ranges), row_blocks * col_blocks))],
        name="compress",
    )(filled, psi)


class Layout:
    def __init__(self, places, row_blocks, col_blocks, terms, chunks):
        self.places, self.row_blocks, self.col_blocks, self.terms, self.chunks = places, row_blocks, col_blocks, terms, chunks
        self.slots = row_blocks * col_blocks
        self.states = places.y * row_blocks
        self.old_right = places.cols * col_blocks
        self.shards = places.y * places.z * places.x
        self.stride = self.old_right + CHUNK
        self.pairs = self.states * terms + GROUP
        self.tile = 2 if col_blocks % 2 == 0 else 1
        self.tiles = col_blocks // self.tile
        self.new_left = CORES * row_blocks
        self.trash = self.new_left
        self.items = self.tiles * ((self.new_left + 1) // 2) + ITEMS
        self.runs = []
        slot, place = 0, 1
        for wide in chunks:
            self.runs.append((slot, wide, place))
            slot += wide
            place += wide * self.shards

    def room(self, chunks):
        return 1 + self.shards * sum(self.chunks[:chunks])

    def shapes(self):
        return [
            (self.states + 1,),
            ((self.states + 1) * self.stride,),
            ((self.states + 1) * self.stride,),
            (2 * self.pairs,),
            (2 * self.pairs,),
            (2 * self.items,),
            (self.items,),
            (3,),
        ]


def plan_kernel(lay, filled, terms, counts, spots, blocks, pair_q, pair_t, lefts, item_tile, totals, used, ready):
    pz, px, py = lay.places.z, lay.places.x, lay.places.y
    row, col = lax.axis_index("row"), lax.axis_index("col")
    core, y_me = row % CORES, row // CORES
    z_me, x_me = col // px, col % px

    def one_state(q, n_ready):
        y = q // lay.row_blocks
        kb = q % lay.row_blocks

        @pl.when(kb == 0)
        def _():
            for dev in range(lay.places.cols):
                used[dev] = 0

        dy = (y_me - y + py) % py
        k_block = (y * CORES + core) * lay.row_blocks + kb
        n = jnp.int32(0)
        most = jnp.int32(0)
        for dev in range(lay.places.cols):
            dz = (z_me - dev // px + pz) % pz
            dx = (x_me - dev % px + px) % px
            shard = (dy * px + dx) * pz + dz
            slot = used[dev]
            for cb in range(lay.col_blocks):
                c = dev * lay.col_blocks + cb
                here = filled[k_block, c]
                spot = jnp.int32(0)
                for first, wide, place in lay.runs:
                    spot = jnp.where(slot >= first, place + shard * wide + slot - first, spot)
                spots[q * lay.stride + n] = spot
                blocks[q * lay.stride + n] = c
                n = n + here
                slot = slot + here
            used[dev] = slot
            most = jnp.maximum(most, slot)

        def pad(i, carry):
            spots[q * lay.stride + i] = 0
            blocks[q * lay.stride + i] = 0
            return carry

        lax.fori_loop(n, lay.stride, pad, 0)
        counts[q] = n
        early = jnp.where(most <= lay.chunks[0], 1, 0)
        ready[q] = early
        for t in range(lay.terms):
            n_ready = n_ready + jnp.where((terms[t, k_block] != 0) & (n > 0), early, 0)
        return n_ready

    n_ready = lax.fori_loop(0, lay.states, one_state, jnp.int32(0))
    n_ready = n_ready // GROUP * GROUP
    n_early, n_late = jnp.int32(0), jnp.int32(0)
    for t in range(lay.terms):

        def one_pair(q, carry):
            n_early, n_late = carry
            k_block = (q // lay.row_blocks * CORES + core) * lay.row_blocks + q % lay.row_blocks
            on = jnp.where((terms[t, k_block] != 0) & (counts[q] > 0), 1, 0)
            early = jnp.where((ready[q] != 0) & (n_early < n_ready), on, 0)
            at = jnp.where(early != 0, n_early, lay.pairs + n_late)
            pair_q[at] = q
            pair_t[at] = t
            return n_early + early, n_late + on - early

        n_early, n_late = lax.fori_loop(0, lay.states, one_pair, (n_early, n_late))
    counts[lay.states] = 0

    def pad_state(i, carry):
        spots[lay.states * lay.stride + i] = 0
        blocks[lay.states * lay.stride + i] = 0
        return carry

    lax.fori_loop(0, lay.stride, pad_state, 0)
    for i in range(GROUP):
        pair_q[lay.pairs + n_late + i] = lay.states
        pair_t[lay.pairs + n_late + i] = lay.terms - 1
    totals[0] = n_early // GROUP
    totals[1] = (n_late + GROUP - 1) // GROUP
    items = jnp.int32(0)
    for tile in range(lay.tiles):
        n = jnp.int32(0)
        for a in range(lay.new_left):
            side, ab = a // lay.row_blocks, a % lay.row_blocks
            a_block = (y_me * CORES + (core + side) % CORES) * lay.row_blocks + ab
            some = jnp.int32(0)
            for i in range(lay.tile):
                some = some | filled[a_block, col * lay.col_blocks + tile * lay.tile + i]
            lefts[2 * items + n] = a
            item_tile[items + n // 2] = tile
            n = n + some
        lefts[2 * items + n] = lay.trash
        items = items + (n + 1) // 2
    for i in range(ITEMS):
        lefts[2 * (items + i)] = lay.trash
        lefts[2 * (items + i) + 1] = lay.trash
        item_tile[items + i] = 0
    totals[2] = (items + ITEMS - 1) // ITEMS


def plan(lay, filled, terms):
    smem = pl.BlockSpec(memory_space=pltpu.SMEM)
    shapes = lay.shapes()
    return pl.pallas_call(
        functools.partial(plan_kernel, lay),
        out_shape=[jax.ShapeDtypeStruct(s, jnp.int32) for s in shapes],
        in_specs=[smem, smem],
        out_specs=[smem] * len(shapes),
        scratch_shapes=[pltpu.SMEM((lay.places.cols,), jnp.int32), pltpu.SMEM((lay.states,), jnp.int32)],
        name="plan",
    )(filled, terms)


def main_kernel(lay, stage, stages, places_of, rows, *refs):
    late = stage == stages
    n_psi = len(places_of)
    counts, spots, blocks, pair_q, pair_t, lefts, item_tile, totals, right, left, sib = refs[:11]
    psi_in, refs = refs[11 : 11 + n_psi], refs[11 + n_psi :]
    before = None
    if stage > 0:
        before, refs = refs[0], refs[1:]
    if late:
        (out_own, out_sib), refs = refs[:2], refs[2:]
    else:
        out, refs = refs[0], refs[1:]
    right_v, psi_v, left_v, acc, w_hi, w_lo, w_acc, right_sem, psi_sem, left_sem, out_sem = refs
    core = lax.axis_index("row") % CORES
    list_at = lay.pairs if late else 0
    everything = CORES * rows

    def left_copies(g, slot, act):
        for i in range(GROUP):
            q = jnp.minimum(pair_q[list_at + g * GROUP + i], lay.states - 1)
            t = pair_t[list_at + g * GROUP + i]
            y, kb = q // lay.row_blocks, q % lay.row_blocks
            at = pl.ds(pl.multiple_of(((y * CORES + core) * lay.row_blocks + kb) * BLOCK, BLOCK), BLOCK)
            lanes = pl.ds(i * BLOCK, BLOCK)
            for side, source in enumerate((left, sib)):
                act(
                    pltpu.make_async_copy(
                        source.at[t, :, at], left_v.at[slot, pl.ds(side * rows, rows), lanes], left_sem.at[slot, 2 * i + side]
                    )
                )

    def right_copy(t):
        return pltpu.make_async_copy(right.at[t], right_v.at[t], right_sem.at[t])

    if late:
        start, stop = 0, totals[1]
    else:
        start, stop = totals[0] * stage // stages, totals[0] * (stage + 1) // stages
    loads = []
    for i, (first, place, wide) in enumerate(places_of):
        loads.append(pltpu.make_async_copy(psi_in[i].at[pl.ds(first, wide)], psi_v.at[pl.ds(place, wide)], psi_sem.at[i]))
    for load in loads:
        load.start()
    if stage > 0:
        sums = pltpu.make_async_copy(before, acc.at[pl.ds(0, everything)], out_sem.at[0])
    first_t = pair_t[list_at + start * GROUP]
    last_t = pair_t[list_at + jnp.maximum(stop * GROUP - 1, 0)]

    @pl.when(stop > start)
    def _():
        right_copy(first_t).start()
        left_copies(start, start % 2, lambda c: c.start())

    psi_v[0] = jnp.zeros((BLOCK, BLOCK), psi_v.dtype)
    if stage > 0:
        sums.start()
        acc[pl.ds(everything, BLOCK), :] = jnp.zeros((BLOCK, acc.shape[1]), acc.dtype)
    else:
        acc[...] = jnp.zeros_like(acc)
    for load in loads:
        load.wait()

    def one_group(g, next_t):
        slot = g % 2
        need_t = pair_t[list_at + g * GROUP + GROUP - 1]

        def one_term(t, carry):
            right_copy(t).wait()

            @pl.when(t < last_t)
            def _():
                right_copy(t + 1).start()

            return carry

        lax.fori_loop(next_t, need_t + 1, one_term, 0)

        @pl.when(g + 1 < stop)
        def _():
            left_copies(g + 1, 1 - slot, lambda c: c.start())

        for low in range(0, GROUP, SIDE):
            qs = [pair_q[list_at + g * GROUP + low + i] for i in range(SIDE)]
            ts = [pair_t[list_at + g * GROUP + low + i] for i in range(SIDE)]
            longest = counts[qs[0]]
            for q in qs[1:]:
                longest = jnp.maximum(longest, counts[q])
            w_acc[...] = jnp.zeros_like(w_acc)

            def one_chunk(j, c1):
                for i in range(SIDE):
                    at = qs[i] * lay.stride + j * CHUNK
                    lhs = jnp.concatenate([psi_v[spots[at + m]] for m in range(CHUNK)], axis=1)
                    rhs = jnp.concatenate(
                        [
                            right_v[ts[i], pl.ds(pl.multiple_of(blocks[at + m] * BLOCK, BLOCK), BLOCK), :]
                            for m in range(CHUNK)
                        ],
                        axis=0,
                    )
                    w_acc[i * BLOCK : (i + 1) * BLOCK, :] += jnp.dot(lhs, rhs, preferred_element_type=jnp.float32)
                return c1

            lax.fori_loop(0, (longest + CHUNK - 1) // CHUNK, one_chunk, 0)
            whole = w_acc[...]
            hi = whole.astype(jnp.bfloat16)
            w_hi[low * BLOCK : (low + SIDE) * BLOCK, :] = hi
            w_lo[low * BLOCK : (low + SIDE) * BLOCK, :] = (whole - hi.astype(jnp.float32)).astype(jnp.bfloat16)
        left_copies(g, slot, lambda c: c.wait())
        if stage > 0:

            @pl.when(g == start)
            def _():
                sums.wait()


        def some_items(m, c0):
            for j in range(ITEMS):
                item = m * ITEMS + j
                width = lay.tile * BLOCK
                lanes = pl.ds(pl.multiple_of(item_tile[item] * width, width), width)
                a = [lefts[2 * item + i] for i in range(2)]
                source = [pl.multiple_of(jnp.minimum(b, lay.new_left - 1) * BLOCK, BLOCK) for b in a]
                lhs = jnp.concatenate([left_v[slot, pl.ds(b, BLOCK), :] for b in source], axis=0)
                gain = jnp.dot(lhs, w_hi[:, lanes], preferred_element_type=jnp.float32)
                gain = gain + jnp.dot(lhs, w_lo[:, lanes], preferred_element_type=jnp.float32)
                for i in range(2):
                    acc[pl.ds(pl.multiple_of(a[i] * BLOCK, BLOCK), BLOCK), lanes] += gain[i * BLOCK : (i + 1) * BLOCK]
            return c0

        lax.fori_loop(0, totals[2], some_items, 0)
        return jnp.maximum(next_t, need_t + 1)

    lax.fori_loop(start, stop, one_group, first_t)
    if stage > 0:

        @pl.when(stop <= start)
        def _():
            sums.wait()

    if late:
        stores = [
            pltpu.make_async_copy(acc.at[pl.ds(rows, rows)], out_sib, out_sem.at[1]),
            pltpu.make_async_copy(acc.at[pl.ds(0, rows)], out_own, out_sem.at[0]),
        ]
    else:
        stores = [pltpu.make_async_copy(acc.at[pl.ds(0, everything)], out, out_sem.at[0])]
    for store in stores:
        store.start()
    for store in stores:
        store.wait()


def contract(lay, stage, stages, tables, right, left, sib, parts, before=None):
    late = stage == stages
    rows = lay.row_blocks * BLOCK
    cols = lay.col_blocks * BLOCK
    flat, places_of = [], []
    for (_, wide, place), part in zip(lay.runs, parts):
        for shard, array, first, count in part:
            flat.append(array)
            places_of.append((first, place + shard * wide, count))
    smem = pl.BlockSpec(memory_space=pltpu.SMEM)
    hbm = pl.BlockSpec(memory_space=pl.ANY)
    operands = [right, left, sib, *flat] + ([before] if stage > 0 else [])
    one = jax.ShapeDtypeStruct((rows, cols), jnp.float32)
    both = jax.ShapeDtypeStruct((CORES * rows, cols), jnp.float32)
    return pl.pallas_call(
        functools.partial(main_kernel, lay, stage, stages, places_of, rows),
        out_shape=[one, one] if late else both,
        in_specs=[smem] * len(tables) + [hbm] * len(operands),
        out_specs=[hbm, hbm] if late else hbm,
        scratch_shapes=[
            pltpu.VMEM(right.shape, jnp.bfloat16),
            pltpu.VMEM((lay.room(len(parts)), BLOCK, BLOCK), jnp.bfloat16),
            pltpu.VMEM((2, CORES * rows, GROUP * BLOCK), jnp.bfloat16),
            pltpu.VMEM((CORES * rows + BLOCK, cols), jnp.float32),
            pltpu.VMEM((GROUP * BLOCK, cols), jnp.bfloat16),
            pltpu.VMEM((GROUP * BLOCK, cols), jnp.bfloat16),
            pltpu.VMEM((SIDE * BLOCK, cols), jnp.float32),
            pltpu.SemaphoreType.DMA((lay.terms,)),
            pltpu.SemaphoreType.DMA((len(flat),)),
            pltpu.SemaphoreType.DMA((2, 2 * GROUP)),
            pltpu.SemaphoreType.DMA((2,)),
        ],
        compiler_params=pltpu.CompilerParams(vmem_limit_bytes=VMEM_LIMIT),
        cost_estimate=pl.CostEstimate(
            flops=2 * right.shape[0] * rows * right.shape[1] * cols, bytes_accessed=right.size * 4, transcendentals=0
        ),
        name="late_contract" if late else "early_contract",
    )(*tables, *operands)


def pack_kernel(copies, *refs):
    n_out = 1 + max(copy[3] for copy in copies)
    sources, outs, sems = refs[: -1 - n_out], refs[-1 - n_out : -1], refs[-1]
    moves = [
        pltpu.make_async_copy(sources[source].at[pl.ds(first, wide)], outs[out].at[pl.ds(at, wide)], sems.at[i])
        for i, (source, first, wide, out, at) in enumerate(copies)
    ]
    for move in moves:
        move.start()
    for move in moves:
        move.wait()


def pack(arrays, copies):
    n_out = 1 + max(copy[3] for copy in copies)
    sizes = [sum(copy[2] for copy in copies if copy[3] == out) for out in range(n_out)]
    vmem = pl.BlockSpec(memory_space=pltpu.VMEM)
    return pl.pallas_call(
        functools.partial(pack_kernel, copies),
        out_shape=[jax.ShapeDtypeStruct((size, *arrays[0].shape[1:]), arrays[0].dtype) for size in sizes],
        in_specs=[vmem] * len(arrays),
        out_specs=[vmem] * n_out,
        scratch_shapes=[pltpu.SemaphoreType.DMA((len(copies),))],
        name="pack",
    )(*arrays)


def after(array, *others):
    return lax.optimization_barrier((array, *others))[0]


class Spread:
    def __init__(self, places, part, x_own, y_own, first):
        self.places, self.part, self.wide = places, part, part.shape[0]
        self.x_own, self.y_own, self.first = x_own, y_own, first

    def over_z(self, *others):
        part = after(self.part, *others) if others else self.part
        z = self.places.z
        up, down = {0: part}, {0: part}
        for far in range(1, z // 2 + 1):
            up[far] = move(self.places, up[far - 1], dz=1)
            if far < z - far:
                down[far] = move(self.places, down[far - 1], dz=z - 1)
        self.z = [up[dz] if dz in up else down[z - dz] for dz in range(1, z)]

    def pack_z(self, *others):
        z = [after(array, *others) for array in self.z] if others else self.z
        (self.q,) = pack(z, [(i, 0, self.wide, 0, i * self.wide) for i in range(len(self.z))])
        return self.q

    def over_xy(self, *others):
        q = after(self.q, *others) if others else self.q
        self.x_line = [move(self.places, q, dx=dx) for dx in range(1, self.places.x)]
        self.y_line = [move(self.places, q, dy=dy) for dy in range(1, self.places.y)]

    def pack_rest(self, *others):
        w, half = self.wide, self.places.z // 2
        n_x, n_y = len(self.x_own), len(self.y_own)
        y_line = [after(array, *others) for array in self.y_line] if others else self.y_line
        arrays = self.x_own + self.x_line + y_line
        copies = []
        for i in range(n_x):
            copies.append((i, self.first, w, i, 0))
            if half > 1:
                copies.append((n_x + i, 0, (half - 1) * w, i, w))
        for i in range(n_y):
            copies.append((2 * n_x + i, (half - 1) * w, (self.places.z - half) * w, n_x + i, 0))
        packed = pack(arrays, copies)
        self.from_x, self.from_y = packed[:n_x], packed[n_x:]
        return self.from_x[0]

    def rest(self):
        self.rest_over_y = {
            (dy, i + 1): move(self.places, array, dy=dy)
            for i, array in enumerate(self.from_x)
            for dy in range(1, self.places.y)
        }
        self.rest_over_x = {
            (i + 1, dx): move(self.places, array, dx=dx)
            for i, array in enumerate(self.from_y)
            for dx in range(1, self.places.x)
        }
        return [*self.rest_over_y.values(), *self.rest_over_x.values()]

    def arrays(self):
        x, z, w = self.places.x, self.places.z, self.wide
        got = [(0, self.part, 0, w), (1, self.q, 0, (z - 1) * w)]
        for own, line, step in ((self.x_own, self.x_line, z), (self.y_own, self.y_line, x * z)):
            for i in range(len(own)):
                got.append(((i + 1) * step, own[i], self.first, w))
                got.append(((i + 1) * step + 1, line[i], 0, (z - 1) * w))
        for (dy, dx), array in self.rest_over_y.items():
            got.append(((dy * x + dx) * z, array, 0, array.shape[0]))
        for (dy, dx), array in self.rest_over_x.items():
            got.append(((dy * x + dx) * z + z // 2, array, 0, array.shape[0]))
        return got


def move(places, array, **step):
    return lax.ppermute(array, AXES, places.shift(**step))


def on_device(wavefunction, left_env, right_env, filled_blocks, term_columns):
    rows, cols = wavefunction.shape
    row_blocks, col_blocks = rows // BLOCK, cols // BLOCK
    places = Places(lax.axis_size("row"), lax.axis_size("col"))
    slots = row_blocks * col_blocks
    chunks = [-(-slots * 10 // 32), slots * 8 // 32]
    base = sum(chunks)
    chunks.append(slots - base)
    lay = Layout(places, row_blocks, col_blocks, left_env.shape[0], chunks)
    row_place, col_place = lax.axis_index("row"), lax.axis_index("col")

    own, part1, part2, part3 = compress(
        wavefunction, filled_blocks, [(0, base), (0, chunks[0]), (chunks[0], base), (base, slots)]
    )
    x_own = [move(places, own, dx=dx) for dx in range(1, places.x)]
    y_own = [move(places, own, dy=dy) for dy in range(1, places.y)]
    one = Spread(places, part1, x_own, y_own, 0)
    two = Spread(places, part2, x_own, y_own, chunks[0])

    one.over_z()
    one.pack_z(*x_own, *y_own)
    one.over_xy()
    two.over_z(one.q)
    swap = places.shift(dcore=1)
    sib = lax.ppermute(left_env, AXES, swap)
    tables = plan(lay, filled_blocks, term_columns)
    two.pack_z()
    one.pack_rest(two.q)
    diagonal = one.rest()
    first = one.arrays()
    two.q = after(two.q, *diagonal)
    two.over_xy()
    early = contract(lay, 0, 2, tables, after(right_env, two.q), left_env, sib, [first])
    gone = two.pack_rest(early)
    two.rest()
    early = contract(lay, 1, 2, tables, after(right_env, gone), left_env, sib, [first], early)
    second = two.arrays()

    per_device = filled_blocks.reshape(places.rows, row_blocks, places.cols, col_blocks).sum(axis=(1, 3))

    def more(_):
        three = Spread(
            places,
            part3,
            [move(places, part3, dx=dx) for dx in range(1, places.x)],
            [move(places, part3, dy=dy) for dy in range(1, places.y)],
            0,
        )
        three.over_z()
        three.pack_z()
        three.over_xy()
        three.pack_rest()
        three.rest()
        return contract(lay, 2, 2, tables, right_env, left_env, sib, [first, second, three.arrays()], early)

    def enough(_):
        return contract(lay, 2, 2, tables, right_env, left_env, sib, [first, second], early)

    own, theirs = lax.cond(jnp.max(per_device) > base, more, enough, 0)
    summed = own + lax.ppermute(theirs, AXES, swap)
    here = lax.dynamic_slice(
        filled_blocks, (row_place * row_blocks, col_place * col_blocks), (row_blocks, col_blocks)
    )
    result = jnp.where(
        here[:, None, :, None] != 0, summed.reshape(row_blocks, BLOCK, col_blocks, BLOCK), jnp.float32(0)
    )
    return result.reshape(rows, cols).astype(jnp.bfloat16)


def solution(mesh):
    in_specs = (P("row", "col"), P(None, "row", None), P(None, None, "col"), P(), P())
    out_specs = P("row", "col")
    return jax.shard_map(
        on_device, mesh=mesh, in_specs=in_specs, out_specs=out_specs, check_vma=False
    )
```

profile of v0, /device:TPU:0, one launch (start us, length us, event | category | flops | bytes accessed | tf_op | source)
XLA Modules:
  0.0 174.2 jit_solution(9236190302190127692)
XLA Ops:
  0.5 4.7 %compress.1 = (bf16[18,128,128]{2,1,0:T(8,128)(2,1)}, bf16[10,128,128]{2,1,0:T(8,128)(2,1)}, bf16[8,128,128]{2,1,0:T(8,128)(2,1)}, bf16[14,128,128]{2,1,0:T(8,128)(2,1)}) custom-call(s32[32,32]{1,0:T(8,128)} %filled.3, bf16[1024,512]{1,0:T(8,128)(2,1)} %psi.1), custom_call_target="tpu_custom_call" | custom-call | tf_op jit(solution)/shard_map/compress/pallas_call | solution.py:73
  5.1 2.6 %collective-permute-start.10 = (bf16[10,128,128]{2,1,0:T(8,128)(2,1)}, bf16[10,128,128]{2,1,0:T(8,128)(2,1)S(1)}, u32[]{:S(2)}, u32[]{:S(2)}) collective-permute-start(bf16[10,128,128]{2,1,0:T(8,128)(2,1)} %get-tuple-element.201.refs_11_), channel_id=1, source_target_pairs={{0,2},{1,3},{2,4},{3,5},{4,6},{5,7},{6,0},{7,1},{8,10},{9,11},{10,... | collective-permute-start | bytes 983048 | tf_op jit(solution)/shard_map/ppermute | solution.py:526
  7.7 1.5 collective-permute-start.11
  9.3 1.5 collective-permute-start.12
  10.7 2.2 %collective-permute-start.14 = (bf16[10,128,128]{2,1,0:T(8,128)(2,1)}, bf16[10,128,128]{2,1,0:T(8,128)(2,1)S(1)}, u32[]{:S(2)}, u32[]{:S(2)}) collective-permute-start(bf16[10,128,128]{2,1,0:T(8,128)(2,1)} %get-tuple-element.201.refs_11_), channel_id=1, source_target_pairs={{0,6},{1,7},{2,0},{3,1},{4,2},{5,3},{6,4},{7,5},{8,14},{9,15},{10,... | collective-permute-start | bytes 983048 | tf_op jit(solution)/shard_map/ppermute | solution.py:526
  13.0 5.6 %collective-permute-done.10.refs_0_ = bf16[10,128,128]{2,1,0:T(8,128)(2,1)S(1)} collective-permute-done((bf16[10,128,128]{2,1,0:T(8,128)(2,1)}, bf16[10,128,128]{2,1,0:T(8,128)(2,1)S(1)}, u32[]{:S(2)}, u32[]{:S(2)}) %collective-permute-start.10) | collective-permute-done | bytes 327712 | tf_op jit(solution)/shard_map/ppermute | solution.py:526
  18.6 4.9 %collective-permute-done.11.refs_0_.refs_13_ = bf16[18,128,128]{2,1,0:T(8,128)(2,1)S(1)} collective-permute-done((bf16[18,128,128]{2,1,0:T(8,128)(2,1)}, bf16[18,128,128]{2,1,0:T(8,128)(2,1)S(1)}, u32[]{:S(2)}, u32[]{:S(2)}) %collective-permute-start.11) | collective-permute-done | bytes 589856 | tf_op jit(solution)/shard_map/ppermute | solution.py:526
  23.4 1.3 collective-permute-done.12.refs_15_
  25.5 7.0 %collective-permute-done.13.refs_1_ = bf16[10,128,128]{2,1,0:T(8,128)(2,1)S(1)} collective-permute-done((bf16[10,128,128]{2,1,0:T(8,128)(2,1)S(1)}, bf16[10,128,128]{2,1,0:T(8,128)(2,1)S(1)}, u32[]{:S(2)}, u32[]{:S(2)}) %collective-permute-start.13) | collective-permute-done | bytes 327712 | tf_op jit(solution)/shard_map/ppermute | solution.py:526
  33.2 1.5 pack.8.refs_12_
  34.7 1.6 collective-permute-start.16
  36.3 1.5 collective-permute-start.15
  37.8 3.8 %collective-permute-start.19 = (bf16[8,128,128]{2,1,0:T(8,128)(2,1)}, bf16[8,128,128]{2,1,0:T(8,128)(2,1)}, u32[]{:S(2)}, u32[]{:S(2)}) collective-permute-start(bf16[8,128,128]{2,1,0:T(8,128)(2,1)} %get-tuple-element.207), channel_id=1, source_target_pairs={{0,6},{1,7},{2,0},{3,1},{4,2},{5,3},{6,4},{7,5},{8,14},{9,15},{10,... | collective-permute-start | bytes 786440 | tf_op jit(solution)/shard_map/ppermute | solution.py:526
  41.6 6.5 %collective-permute-done.17.refs_0_ = bf16[8,128,128]{2,1,0:T(8,128)(2,1)S(1)} collective-permute-done((bf16[8,128,128]{2,1,0:T(8,128)(2,1)}, bf16[8,128,128]{2,1,0:T(8,128)(2,1)S(1)}, u32[]{:S(2)}, u32[]{:S(2)}) %collective-permute-start.17) | collective-permute-done | bytes 262176 | tf_op jit(solution)/shard_map/ppermute | solution.py:526
  48.8 4.3 %collective-permute-done.19.refs_2_ = bf16[8,128,128]{2,1,0:T(8,128)(2,1)} collective-permute-done((bf16[8,128,128]{2,1,0:T(8,128)(2,1)}, bf16[8,128,128]{2,1,0:T(8,128)(2,1)}, u32[]{:S(2)}, u32[]{:S(2)}) %collective-permute-start.19) | collective-permute-done | bytes 262176 | tf_op jit(solution)/shard_map/ppermute | solution.py:526
  53.2 3.9 %collective-permute-done.18.refs_1_ = bf16[8,128,128]{2,1,0:T(8,128)(2,1)} collective-permute-done((bf16[8,128,128]{2,1,0:T(8,128)(2,1)S(1)}, bf16[8,128,128]{2,1,0:T(8,128)(2,1)}, u32[]{:S(2)}, u32[]{:S(2)}) %collective-permute-start.18) | collective-permute-done | bytes 262176 | tf_op jit(solution)/shard_map/ppermute | solution.py:526
  57.1 2.1 %pack.9 = bf16[24,128,128]{2,1,0:T(8,128)(2,1)} custom-call(bf16[8,128,128]{2,1,0:T(8,128)(2,1)} %copy-done.7, bf16[8,128,128]{2,1,0:T(8,128)(2,1)} %collective-permute-done.18.refs_1_, bf16[8,128,128]{2,1,0:T(8,128)(2,1)} %collective-permute-done.19.refs_2_), custom_call_target="tpu_custom_call" | custom-call | tf_op jit(solution)/shard_map/pack/pallas_call | solution.py:443
  59.2 1.5 pack.10
  62.3 10.5 %plan.1 = (s32[17]{0:T(128)}, s32[680]{0:T(1024)S(1)}, s32[680]{0:T(1024)S(1)}, s32[144]{0:T(256)S(1)}, s32[144]{0:T(256)}, /*index=5*/s32[36]{0:T(128)}, s32[18]{0:T(128)}, s32[3]{0:T(128)}) custom-call(s32[32,32]{1,0:T(8,128)} %filled.3, s32[4,32]{1,0:T(4,128)} %terms.1), custom_call_target="tpu_custom_call" | custom-call | tf_op jit(solution)/shard_map/plan/pallas_call | solution.py:223
  72.9 1.4 reshape.8
  74.3 1.1 reduce_sum.9
  76.6 1.6 collective-permute-start.23
  78.2 1.7 collective-permute-start.22
  79.9 22.3 %early_contract.2.refs_19_ = f32[2048,512]{1,0:T(8,128)} custom-call(s32[17]{0:T(128)} %get-tuple-element.193.refs_0_, s32[680]{0:T(1024)S(1)} %get-tuple-element.194.refs_1_, s32[680]{0:T(1024)S(1)} %get-tuple-element.195.refs_2_, s32[144]{0:T(256)S(1)} %get-tuple-element.196.refs_3_, s32[144]{0:T(256)} %get-tuple-element.197.refs_4_, ...), custom_call_target="tpu_custom_call" | custom-call | flops 17179869184 | bytes 33554432 | tf_op jit(solution)/shard_map/early_contract/pallas_call | solution.py:400
  102.2 2.4 %pack.11 = (bf16[16,128,128]{2,1,0:T(8,128)(2,1)}, bf16[16,128,128]{2,1,0:T(8,128)(2,1)}) custom-call(bf16[18,128,128]{2,1,0:T(8,128)(2,1)S(1)} %collective-permute-done.11.refs_0_.refs_13_, bf16[24,128,128]{2,1,0:T(8,128)(2,1)} %collective-permute-done.22.refs_1_, bf16[24,128,128]{2,1,0:T(8,128)(2,1)} %collective-permute-done.23.refs_2_), custom_call_target="tpu_custom_call" | custom-call | tf_op jit(solution)/shard_map/pack/pallas_call | solution.py:443
  104.8 2.0 %collective-permute-start.25 = (bf16[16,128,128]{2,1,0:T(8,128)(2,1)}, bf16[16,128,128]{2,1,0:T(8,128)(2,1)}, u32[]{:S(2)}, u32[]{:S(2)}) collective-permute-start(bf16[16,128,128]{2,1,0:T(8,128)(2,1)} %get-tuple-element.215), channel_id=1, source_target_pairs={{0,1},{1,0},{2,3},{3,2},{4,5},{5,4},{6,7},{7,6},{8,9},{9,8},{10,11... | collective-permute-start | bytes 1572872 | tf_op jit(solution)/shard_map/ppermute | solution.py:526
  106.8 25.2 %early_contract.3 = f32[2048,512]{1,0:T(8,128)} custom-call(s32[17]{0:T(128)} %get-tuple-element.193.refs_0_, s32[680]{0:T(1024)S(1)} %get-tuple-element.194.refs_1_, s32[680]{0:T(1024)S(1)} %get-tuple-element.195.refs_2_, s32[144]{0:T(256)S(1)} %get-tuple-element.196.refs_3_, s32[144]{0:T(256)S(1)} %copy-done.9, s32[36]{0:T(128)} %get-tuple-element.198.refs_5_, ...), custom_call_target="tpu_custom_call" | custom-call | flops 17179869184 | bytes 33554432 | tf_op jit(solution)/shard_map/early_contract/pallas_call | solution.py:400
  132.0 34.2 %conditional.1 = ((f32[1024,512]{1,0:T(8,128)}, f32[1024,512]{1,0:T(8,128)})) conditional(s32[]{:T(128)} %convert_element_type.6, (s32[17]{0:T(128)S(1)}, s32[680]{0:T(1024)S(1)}, s32[680]{0:T(1024)S(1)}, s32[144]{0:T(256)S(1)}, s32[144]{0:T(256)S(1)}, /*index=5*/s32[36]{0:T(128)S(1)}, s32[18]{0:T(128)S(1)}, s32[3]{0:T(128)S(1)}, ...), branch_computations={%region_2.0_spmd, %region_3.0_spmd} | conditional | flops 17179869184 | bytes 72091376 | solution.py:587
  132.0 34.0 %late_contract.2 = (f32[1024,512]{1,0:T(8,128)}, f32[1024,512]{1,0:T(8,128)}) custom-call(s32[17]{0:T(128)S(1)} %get-tuple-element.111.refs_0_, s32[680]{0:T(1024)S(1)} %get-tuple-element.112.refs_1_, s32[680]{0:T(1024)S(1)} %get-tuple-element.113.refs_2_, s32[144]{0:T(256)S(1)} %get-tuple-element.114.refs_3_, s32[144]{0:T(256)S(1)} %get-tuple-element.115.refs_4_, ...), custom_call_target="tpu_custom_call" | custom-call | flops 17179869184 | bytes 33554432 | tf_op jit(solution)/shard_map/cond/branch_0_fun/late_contract/pallas_call | solution.py:400
  166.3 0.8 dynamic-slice_compare_fusion
  167.1 3.6 %collective-permute-done.26 = f32[1024,512]{1,0:T(8,128)S(1)} collective-permute-done((f32[1024,512]{1,0:T(8,128)}, f32[1024,512]{1,0:T(8,128)S(1)}, u32[]{:S(2)}, u32[]{:S(2)}) %collective-permute-start.26) | collective-permute-done | bytes 2097184 | tf_op jit(solution)/shard_map/ppermute | solution.py:588
  171.0 3.2 %select_convert_fusion = bf16[1024,512]{1,0:T(8,128)(2,1)} fusion(f32[1024,512]{1,0:T(8,128)} %get-tuple-element.218, f32[1024,512]{1,0:T(8,128)S(1)} %collective-permute-done.26, pred[128,8,4,128]{3,2,1,0:T(4,128)(4,1)S(1)} %bitcast.6), kind=kLoop, calls=%fused_computation | loop fusion | flops 1572864 | bytes 5767168 | tf_op jit(solution)/shard_map/convert_element_type | solution.py:595
  (41 shorter events, 5.4 us)
Async XLA Ops:
  0.0 79.9 %collective-permute-start.9 = (bf16[4,1024,4096]{2,1,0:T(8,128)(2,1)}, bf16[4,1024,4096]{2,1,0:T(8,128)(2,1)}, u32[]{:S(2)}, u32[]{:S(2)}) collective-permute-start(bf16[4,1024,4096]{2,1,0:T(8,128)(2,1)} %refs_9_.3), channel_id=1, source_target_pairs={{0,8},{1,9},{2,10},{3,11},{4,12},{5,13},{6,14},{7,15},{8,0},{9,1},... | collective-permute-start | bytes 100663304 | tf_op jit(solution)/shard_map/ppermute | solution.py:553
  5.1 13.4 %collective-permute-start.10 = (bf16[10,128,128]{2,1,0:T(8,128)(2,1)}, bf16[10,128,128]{2,1,0:T(8,128)(2,1)S(1)}, u32[]{:S(2)}, u32[]{:S(2)}) collective-permute-start(bf16[10,128,128]{2,1,0:T(8,128)(2,1)} %get-tuple-element.201.refs_11_), channel_id=1, source_target_pairs={{0,2},{1,3},{2,4},{3,5},{4,6},{5,7},{6,0},{7,1},{8,10},{9,11},{10,... | collective-permute-start | bytes 983048 | tf_op jit(solution)/shard_map/ppermute | solution.py:526
  7.7 15.7 %collective-permute-start.11 = (bf16[18,128,128]{2,1,0:T(8,128)(2,1)}, bf16[18,128,128]{2,1,0:T(8,128)(2,1)S(1)}, u32[]{:S(2)}, u32[]{:S(2)}) collective-permute-start(bf16[18,128,128]{2,1,0:T(8,128)(2,1)} %get-tuple-element.202), channel_id=1, source_target_pairs={{0,1},{1,0},{2,3},{3,2},{4,5},{5,4},{6,7},{7,6},{8,9},{9,8},{10,11... | collective-permute-start | bytes 1769480 | tf_op jit(solution)/shard_map/ppermute | solution.py:526
  9.3 15.5 %collective-permute-start.12 = (bf16[18,128,128]{2,1,0:T(8,128)(2,1)}, bf16[18,128,128]{2,1,0:T(8,128)(2,1)}, u32[]{:S(2)}, u32[]{:S(2)}) collective-permute-start(bf16[18,128,128]{2,1,0:T(8,128)(2,1)} %get-tuple-element.202), channel_id=1, source_target_pairs={{0,16},{1,17},{2,18},{3,19},{4,20},{5,21},{6,22},{7,23},{8,24},{9,... | collective-permute-start | bytes 1769480 | tf_op jit(solution)/shard_map/ppermute | solution.py:526
  10.7 14.7 %collective-permute-start.14 = (bf16[10,128,128]{2,1,0:T(8,128)(2,1)}, bf16[10,128,128]{2,1,0:T(8,128)(2,1)S(1)}, u32[]{:S(2)}, u32[]{:S(2)}) collective-permute-start(bf16[10,128,128]{2,1,0:T(8,128)(2,1)} %get-tuple-element.201.refs_11_), channel_id=1, source_target_pairs={{0,6},{1,7},{2,0},{3,1},{4,2},{5,3},{6,4},{7,5},{8,14},{9,15},{10,... | collective-permute-start | bytes 983048 | tf_op jit(solution)/shard_map/ppermute | solution.py:526
  18.6 13.9 %copy-start.4 = (bf16[10,128,128]{2,1,0:T(8,128)(2,1)}, bf16[10,128,128]{2,1,0:T(8,128)(2,1)S(1)}, u32[]{:S(2)}) copy-start(bf16[10,128,128]{2,1,0:T(8,128)(2,1)S(1)} %collective-permute-done.10.refs_0_) | copy-start | bytes 983044
  18.6 13.9 %collective-permute-start.13 = (bf16[10,128,128]{2,1,0:T(8,128)(2,1)S(1)}, bf16[10,128,128]{2,1,0:T(8,128)(2,1)S(1)}, u32[]{:S(2)}, u32[]{:S(2)}) collective-permute-start(bf16[10,128,128]{2,1,0:T(8,128)(2,1)S(1)} %collective-permute-done.10.refs_0_), channel_id=1, source_target_pairs={{0,2},{1,3},{2,4},{3,5},{4,6},{5,7},{6,0},{7,1},{8,10},{9,11},{10,... | collective-permute-start | bytes 983048 | tf_op jit(solution)/shard_map/ppermute | solution.py:526
  25.5 7.0 %copy-start.5 = (bf16[10,128,128]{2,1,0:T(8,128)(2,1)}, bf16[10,128,128]{2,1,0:T(8,128)(2,1)S(1)}, u32[]{:S(2)}) copy-start(bf16[10,128,128]{2,1,0:T(8,128)(2,1)S(1)} %collective-permute-done.14.refs_2_) | copy-start | bytes 983044
  32.5 0.7 copy-start.6
  34.7 27.0 %copy-start.8 = (s32[32,32]{1,0:T(8,128)S(1)}, s32[32,32]{1,0:T(8,128)}, u32[]{:S(2)}) copy-start(s32[32,32]{1,0:T(8,128)} %filled.3) | copy-start | bytes 12292
  34.7 24.5 %collective-permute-start.16 = (bf16[30,128,128]{2,1,0:T(8,128)(2,1)S(1)}, bf16[30,128,128]{2,1,0:T(8,128)(2,1)S(1)}, u32[]{:S(2)}, u32[]{:S(2)}) collective-permute-start(bf16[30,128,128]{2,1,0:T(8,128)(2,1)S(1)} %pack.8.refs_12_), channel_id=1, source_target_pairs={{0,16},{1,17},{2,18},{3,19},{4,20},{5,21},{6,22},{7,23},{8,24},{9,... | collective-permute-start | bytes 2949128 | tf_op jit(solution)/shard_map/ppermute | solution.py:526
  36.3 22.9 %collective-permute-start.15 = (bf16[30,128,128]{2,1,0:T(8,128)(2,1)S(1)}, bf16[30,128,128]{2,1,0:T(8,128)(2,1)S(1)}, u32[]{:S(2)}, u32[]{:S(2)}) collective-permute-start(bf16[30,128,128]{2,1,0:T(8,128)(2,1)S(1)} %pack.8.refs_12_), channel_id=1, source_target_pairs={{0,1},{1,0},{2,3},{3,2},{4,5},{5,4},{6,7},{7,6},{8,9},{9,8},{10,11... | collective-permute-start | bytes 2949128 | tf_op jit(solution)/shard_map/ppermute | solution.py:526
  37.8 10.3 %collective-permute-start.17 = (bf16[8,128,128]{2,1,0:T(8,128)(2,1)}, bf16[8,128,128]{2,1,0:T(8,128)(2,1)S(1)}, u32[]{:S(2)}, u32[]{:S(2)}) collective-permute-start(bf16[8,128,128]{2,1,0:T(8,128)(2,1)} %get-tuple-element.207), channel_id=1, source_target_pairs={{0,2},{1,3},{2,4},{3,5},{4,6},{5,7},{6,0},{7,1},{8,10},{9,11},{10,... | collective-permute-start | bytes 786440 | tf_op jit(solution)/shard_map/ppermute | solution.py:526
  37.8 15.4 %collective-permute-start.19 = (bf16[8,128,128]{2,1,0:T(8,128)(2,1)}, bf16[8,128,128]{2,1,0:T(8,128)(2,1)}, u32[]{:S(2)}, u32[]{:S(2)}) collective-permute-start(bf16[8,128,128]{2,1,0:T(8,128)(2,1)} %get-tuple-element.207), channel_id=1, source_target_pairs={{0,6},{1,7},{2,0},{3,1},{4,2},{5,3},{6,4},{7,5},{8,14},{9,15},{10,... | collective-permute-start | bytes 786440 | tf_op jit(solution)/shard_map/ppermute | solution.py:526
  48.1 0.7 copy-start.7
  48.8 8.3 %collective-permute-start.18 = (bf16[8,128,128]{2,1,0:T(8,128)(2,1)S(1)}, bf16[8,128,128]{2,1,0:T(8,128)(2,1)}, u32[]{:S(2)}, u32[]{:S(2)}) collective-permute-start(bf16[8,128,128]{2,1,0:T(8,128)(2,1)S(1)} %collective-permute-done.17.refs_0_), channel_id=1, source_target_pairs={{0,2},{1,3},{2,4},{3,5},{4,6},{5,7},{6,0},{7,1},{8,10},{9,11},{10,... | collective-permute-start | bytes 786440 | tf_op jit(solution)/shard_map/ppermute | solution.py:526
  60.7 15.8 %collective-permute-start.20 = (bf16[20,128,128]{2,1,0:T(8,128)(2,1)}, bf16[20,128,128]{2,1,0:T(8,128)(2,1)}, u32[]{:S(2)}, u32[]{:S(2)}) collective-permute-start(bf16[20,128,128]{2,1,0:T(8,128)(2,1)} %get-tuple-element.209), channel_id=1, source_target_pairs={{0,16},{1,17},{2,18},{3,19},{4,20},{5,21},{6,22},{7,23},{8,24},{9,... | collective-permute-start | bytes 1966088 | tf_op jit(solution)/shard_map/ppermute | solution.py:526
  61.2 15.3 %collective-permute-start.21 = (bf16[20,128,128]{2,1,0:T(8,128)(2,1)}, bf16[20,128,128]{2,1,0:T(8,128)(2,1)}, u32[]{:S(2)}, u32[]{:S(2)}) collective-permute-start(bf16[20,128,128]{2,1,0:T(8,128)(2,1)} %get-tuple-element.210), channel_id=1, source_target_pairs={{0,1},{1,0},{2,3},{3,2},{4,5},{5,4},{6,7},{7,6},{8,9},{9,8},{10,11... | collective-permute-start | bytes 1966088 | tf_op jit(solution)/shard_map/ppermute | solution.py:526
  76.6 25.6 %collective-permute-start.23 = (bf16[24,128,128]{2,1,0:T(8,128)(2,1)}, bf16[24,128,128]{2,1,0:T(8,128)(2,1)}, u32[]{:S(2)}, u32[]{:S(2)}) collective-permute-start(bf16[24,128,128]{2,1,0:T(8,128)(2,1)} %pack.9), channel_id=1, source_target_pairs={{0,16},{1,17},{2,18},{3,19},{4,20},{5,21},{6,22},{7,23},{8,24},{9,... | collective-permute-start | bytes 2359304 | tf_op jit(solution)/shard_map/ppermute | solution.py:526
  78.2 24.0 %collective-permute-start.22 = (bf16[24,128,128]{2,1,0:T(8,128)(2,1)}, bf16[24,128,128]{2,1,0:T(8,128)(2,1)}, u32[]{:S(2)}, u32[]{:S(2)}) collective-permute-start(bf16[24,128,128]{2,1,0:T(8,128)(2,1)} %pack.9), channel_id=1, source_target_pairs={{0,1},{1,0},{2,3},{3,2},{4,5},{5,4},{6,7},{7,6},{8,9},{9,8},{10,11... | collective-permute-start | bytes 2359304 | tf_op jit(solution)/shard_map/ppermute | solution.py:526
  102.2 4.6 %copy-start.9 = (s32[144]{0:T(256)S(1)}, s32[144]{0:T(256)}, u32[]{:S(2)}) copy-start(s32[144]{0:T(256)} %get-tuple-element.197.refs_4_) | copy-start | bytes 1732
  104.7 27.3 %collective-permute-start.24 = (bf16[16,128,128]{2,1,0:T(8,128)(2,1)}, bf16[16,128,128]{2,1,0:T(8,128)(2,1)}, u32[]{:S(2)}, u32[]{:S(2)}) collective-permute-start(bf16[16,128,128]{2,1,0:T(8,128)(2,1)} %get-tuple-element.214), channel_id=1, source_target_pairs={{0,16},{1,17},{2,18},{3,19},{4,20},{5,21},{6,22},{7,23},{8,24},{9,... | collective-permute-start | bytes 1572872 | tf_op jit(solution)/shard_map/ppermute | solution.py:526
  104.7 27.2 %copy-start.10 = (s32[17]{0:T(128)S(1)}, s32[17]{0:T(128)}, u32[]{:S(2)}) copy-start(s32[17]{0:T(128)} %get-tuple-element.193.refs_0_) | copy-start | bytes 208
  104.8 27.2 %copy-start.12 = (s32[36]{0:T(128)S(1)}, s32[36]{0:T(128)}, u32[]{:S(2)}) copy-start(s32[36]{0:T(128)} %get-tuple-element.198.refs_5_) | copy-start | bytes 436
  104.8 27.2 %copy-start.14 = (s32[18]{0:T(128)S(1)}, s32[18]{0:T(128)}, u32[]{:S(2)}) copy-start(s32[18]{0:T(128)} %get-tuple-element.199.refs_6_) | copy-start | bytes 220
  104.8 27.2 %copy-start.16 = (s32[3]{0:T(128)S(1)}, s32[3]{0:T(128)}, u32[]{:S(2)}) copy-start(s32[3]{0:T(128)} %get-tuple-element.200.refs_7_) | copy-start | bytes 40
  104.8 27.2 %collective-permute-start.25 = (bf16[16,128,128]{2,1,0:T(8,128)(2,1)}, bf16[16,128,128]{2,1,0:T(8,128)(2,1)}, u32[]{:S(2)}, u32[]{:S(2)}) collective-permute-start(bf16[16,128,128]{2,1,0:T(8,128)(2,1)} %get-tuple-element.215), channel_id=1, source_target_pairs={{0,1},{1,0},{2,3},{3,2},{4,5},{5,4},{6,7},{7,6},{8,9},{9,8},{10,11... | collective-permute-start | bytes 1572872 | tf_op jit(solution)/shard_map/ppermute | solution.py:526
  166.3 4.4 %collective-permute-start.26 = (f32[1024,512]{1,0:T(8,128)}, f32[1024,512]{1,0:T(8,128)S(1)}, u32[]{:S(2)}, u32[]{:S(2)}) collective-permute-start(f32[1024,512]{1,0:T(8,128)} %get-tuple-element.219), channel_id=1, source_target_pairs={{0,8},{1,9},{2,10},{3,11},{4,12},{5,13},{6,14},{7,15},{8,0},{9,1},... | collective-permute-start | bytes 6291464 | tf_op jit(solution)/shard_map/ppermute | solution.py:588
where the time goes:
time: 176 us; the launch traced here: 174 us
  Pallas kernels  104 us (59%)
  waiting for transfers between devices  37.8 us (21%)
  starting transfers between devices  21.5 us (12%)
  other arithmetic  5.64 us (3%)
  local copies, waits for them, and re-layouts  3.91 us (2%)
    pallas_call x3, Pallas kernels, contract(): pl.pallas_call(functools.partial(main_kernel, lay, stage, stages, places_...  81.5 us
    ppermute x16, waiting for transfers between devices, move(): return lax.ppermute(array, AXES, places.shift(**step))  34.3 us
    ppermute x16, starting transfers between devices, move(): return lax.ppermute(array, AXES, places.shift(**step))  21 us
    pallas_call x1, Pallas kernels, plan(): pl.pallas_call(functools.partial(plan_kernel, lay), out_shape=[jax.ShapeD...  10.5 us
    pallas_call x4, Pallas kernels, pack(): pl.pallas_call(functools.partial(pack_kernel, copies), out_shape=[jax.Sha...  7.53 us
    pallas_call x1, Pallas kernels, compress(): pl.pallas_call(functools.partial(compress_kernel, ranges, row_blocks, col...  4.66 us
    ppermute x1, waiting for transfers between devices, on_device(): summed = own + lax.ppermute(theirs, AXES, swap)  3.58 us
  transfers between devices with their start and end apart: 18, of which 9 were waited for; matrix products, arithmetic and copies ran while one was open for 3% of the time, Pallas kernels for 39%

commit v1 on v0

--- a/solution.py
+++ b/solution.py
@@ -101,23 +101,42 @@
             slot += wide
             place += wide * self.shards
 
+        self.lengths = [
+            self.states + 1,
+            (self.states + 1) * self.stride,
+            (self.states + 1) * self.stride,
+            2 * self.pairs,
+            2 * self.pairs,
+            2 * self.items,
+            self.items,
+            self.new_left * col_blocks,
+            3,
+        ]
+
     def room(self, chunks):
         return 1 + self.shards * sum(self.chunks[:chunks])
 
-    def shapes(self):
-        return [
-            (self.states + 1,),
-            ((self.states + 1) * self.stride,),
-            ((self.states + 1) * self.stride,),
-            (2 * self.pairs,),
-            (2 * self.pairs,),
-            (2 * self.items,),
-            (self.items,),
-            (3,),
-        ]
-
-
-def plan_kernel(lay, filled, terms, counts, spots, blocks, pair_q, pair_t, lefts, item_tile, totals, used, ready):
+    def lists(self, table):
+        at, lists = 0, []
+        for length in self.lengths:
+            lists.append(List(table, at))
+            at += length
+        return lists
+
+
+class List:
+    def __init__(self, table, at):
+        self.table, self.at = table, at
+
+    def __getitem__(self, i):
+        return self.table[self.at + i]
+
+    def __setitem__(self, i, value):
+        self.table[self.at + i] = jnp.int32(value)
+
+
+def plan_kernel(lay, filled, terms, table, used, ready):
+    counts, spots, blocks, pair_q, pair_t, lefts, item_tile, allowed, totals = lay.lists(table)
     pz, px, py = lay.places.z, lay.places.x, lay.places.y
     row, col = lax.axis_index("row"), lax.axis_index("col")
     core, y_me = row % CORES, row // CORES
@@ -204,7 +223,9 @@
             a_block = (y_me * CORES + (core + side) % CORES) * lay.row_blocks + ab
             some = jnp.int32(0)
             for i in range(lay.tile):
-                some = some | filled[a_block, col * lay.col_blocks + tile * lay.tile + i]
+                here = filled[a_block, col * lay.col_blocks + tile * lay.tile + i]
+                allowed[a * lay.col_blocks + tile * lay.tile + i] = here
+                some = some | here
             lefts[2 * items + n] = a
             item_tile[items + n // 2] = tile
             n = n + some
@@ -219,12 +240,11 @@
 
 def plan(lay, filled, terms):
     smem = pl.BlockSpec(memory_space=pltpu.SMEM)
-    shapes = lay.shapes()
     return pl.pallas_call(
         functools.partial(plan_kernel, lay),
-        out_shape=[jax.ShapeDtypeStruct(s, jnp.int32) for s in shapes],
+        out_shape=jax.ShapeDtypeStruct((sum(lay.lengths),), jnp.int32),
         in_specs=[smem, smem],
-        out_specs=[smem] * len(shapes),
+        out_specs=smem,
         scratch_shapes=[pltpu.SMEM((lay.places.cols,), jnp.int32), pltpu.SMEM((lay.states,), jnp.int32)],
         name="plan",
     )(filled, terms)
@@ -233,8 +253,9 @@
 def main_kernel(lay, stage, stages, places_of, rows, *refs):
     late = stage == stages
     n_psi = len(places_of)
-    counts, spots, blocks, pair_q, pair_t, lefts, item_tile, totals, right, left, sib = refs[:11]
-    psi_in, refs = refs[11 : 11 + n_psi], refs[11 + n_psi :]
+    table, right, left, sib = refs[:4]
+    counts, spots, blocks, pair_q, pair_t, lefts, item_tile, allowed, totals = lay.lists(table)
+    psi_in, refs = refs[4 : 4 + n_psi], refs[4 + n_psi :]
     before = None
     if stage > 0:
         before, refs = refs[0], refs[1:]
@@ -281,16 +302,21 @@
     @pl.when(stop > start)
     def _():
         right_copy(first_t).start()
-        left_copies(start, start % 2, lambda c: c.start())
 
     psi_v[0] = jnp.zeros((BLOCK, BLOCK), psi_v.dtype)
     if stage > 0:
-        sums.start()
         acc[pl.ds(everything, BLOCK), :] = jnp.zeros((BLOCK, acc.shape[1]), acc.dtype)
     else:
         acc[...] = jnp.zeros_like(acc)
     for load in loads:
         load.wait()
+
+    @pl.when(stop > start)
+    def _():
+        left_copies(start, start % 2, lambda c: c.start())
+
+    if stage > 0:
+        sums.start()
 
     def one_group(g, next_t):
         slot = g % 2
@@ -371,6 +397,12 @@
             sums.wait()
 
     if late:
+        for a in range(lay.new_left):
+            for cb in range(lay.col_blocks):
+                @pl.when(allowed[a * lay.col_blocks + cb] == 0)
+                def _():
+                    acc[pl.ds(a * BLOCK, BLOCK), pl.ds(cb * BLOCK, BLOCK)] = jnp.zeros((BLOCK, BLOCK), acc.dtype)
+
         stores = [
             pltpu.make_async_copy(acc.at[pl.ds(rows, rows)], out_sib, out_sem.at[1]),
             pltpu.make_async_copy(acc.at[pl.ds(0, rows)], out_own, out_sem.at[0]),
@@ -383,7 +415,7 @@
         store.wait()
 
 
-def contract(lay, stage, stages, tables, right, left, sib, parts, before=None):
+def contract(lay, stage, stages, table, right, left, sib, parts, before=None):
     late = stage == stages
     rows = lay.row_blocks * BLOCK
     cols = lay.col_blocks * BLOCK
@@ -400,7 +432,7 @@
     return pl.pallas_call(
         functools.partial(main_kernel, lay, stage, stages, places_of, rows),
         out_shape=[one, one] if late else both,
-        in_specs=[smem] * len(tables) + [hbm] * len(operands),
+        in_specs=[smem] + [hbm] * len(operands),
         out_specs=[hbm, hbm] if late else hbm,
         scratch_shapes=[
             pltpu.VMEM(right.shape, jnp.bfloat16),
@@ -420,7 +452,7 @@
             flops=2 * right.shape[0] * rows * right.shape[1] * cols, bytes_accessed=right.size * 4, transcendentals=0
         ),
         name="late_contract" if late else "early_contract",
-    )(*tables, *operands)
+    )(table, *operands)
 
 
 def pack_kernel(copies, *refs):
@@ -531,68 +563,61 @@
     row_blocks, col_blocks = rows // BLOCK, cols // BLOCK
     places = Places(lax.axis_size("row"), lax.axis_size("col"))
     slots = row_blocks * col_blocks
-    chunks = [-(-slots * 10 // 32), slots * 8 // 32]
-    base = sum(chunks)
-    chunks.append(slots - base)
+    chunks = [-(-slots * 10 // 32), -(-slots * 10 // 32), slots * 4 // 32]
+    base = chunks[0] + chunks[1]
+    chunks.append(slots - sum(chunks))
     lay = Layout(places, row_blocks, col_blocks, left_env.shape[0], chunks)
-    row_place, col_place = lax.axis_index("row"), lax.axis_index("col")
-
-    own, part1, part2, part3 = compress(
-        wavefunction, filled_blocks, [(0, base), (0, chunks[0]), (chunks[0], base), (base, slots)]
-    )
+
+    own, part1, part2 = compress(wavefunction, filled_blocks, [(0, base), (0, chunks[0]), (chunks[0], base)])
     x_own = [move(places, own, dx=dx) for dx in range(1, places.x)]
     y_own = [move(places, own, dy=dy) for dy in range(1, places.y)]
     one = Spread(places, part1, x_own, y_own, 0)
     two = Spread(places, part2, x_own, y_own, chunks[0])
+    swap = places.shift(dcore=1)
+    sib = lax.ppermute(left_env, AXES, swap)
+    table = plan(lay, filled_blocks, term_columns)
+    most = jnp.max(filled_blocks.reshape(places.rows, row_blocks, places.cols, col_blocks).sum(axis=(1, 3)))
 
     one.over_z()
     one.pack_z(*x_own, *y_own)
+    one.q, table, most = lax.optimization_barrier((one.q, table, most))
     one.over_xy()
     two.over_z(one.q)
-    swap = places.shift(dcore=1)
-    sib = lax.ppermute(left_env, AXES, swap)
-    tables = plan(lay, filled_blocks, term_columns)
     two.pack_z()
     one.pack_rest(two.q)
     diagonal = one.rest()
     first = one.arrays()
     two.q = after(two.q, *diagonal)
     two.over_xy()
-    early = contract(lay, 0, 2, tables, after(right_env, two.q), left_env, sib, [first])
+    early = contract(lay, 0, 2, table, after(right_env, two.q), left_env, sib, [first])
     gone = two.pack_rest(early)
     two.rest()
-    early = contract(lay, 1, 2, tables, after(right_env, gone), left_env, sib, [first], early)
+    early = contract(lay, 1, 2, table, after(right_env, gone), left_env, sib, [first], early)
     second = two.arrays()
 
-    per_device = filled_blocks.reshape(places.rows, row_blocks, places.cols, col_blocks).sum(axis=(1, 3))
-
-    def more(_):
-        three = Spread(
-            places,
-            part3,
-            [move(places, part3, dx=dx) for dx in range(1, places.x)],
-            [move(places, part3, dy=dy) for dy in range(1, places.y)],
-            0,
-        )
-        three.over_z()
-        three.pack_z()
-        three.over_xy()
-        three.pack_rest()
-        three.rest()
-        return contract(lay, 2, 2, tables, right_env, left_env, sib, [first, second, three.arrays()], early)
-
-    def enough(_):
-        return contract(lay, 2, 2, tables, right_env, left_env, sib, [first, second], early)
-
-    own, theirs = lax.cond(jnp.max(per_device) > base, more, enough, 0)
-    summed = own + lax.ppermute(theirs, AXES, swap)
-    here = lax.dynamic_slice(
-        filled_blocks, (row_place * row_blocks, col_place * col_blocks), (row_blocks, col_blocks)
-    )
-    result = jnp.where(
-        here[:, None, :, None] != 0, summed.reshape(row_blocks, BLOCK, col_blocks, BLOCK), jnp.float32(0)
-    )
-    return result.reshape(rows, cols).astype(jnp.bfloat16)
+    def finish(extra, _):
+        low, parts = base, [first, second]
+        for wide in chunks[2 : 2 + extra]:
+            (part,) = compress(wavefunction, filled_blocks, [(low, low + wide)])
+            more = Spread(
+                places,
+                part,
+                [move(places, part, dx=dx) for dx in range(1, places.x)],
+                [move(places, part, dy=dy) for dy in range(1, places.y)],
+                0,
+            )
+            more.over_z()
+            more.pack_z()
+            more.over_xy()
+            more.pack_rest()
+            more.rest()
+            parts.append(more.arrays())
+            low += wide
+        return contract(lay, 2, 2, table, right_env, left_env, sib, parts, early)
+
+    levels = jnp.where(most > base, 1, 0) + jnp.where(most > base + chunks[2], 1, 0)
+    own, theirs = lax.switch(levels, [functools.partial(finish, extra) for extra in range(3)], 0)
+    return (own + lax.ppermute(theirs, AXES, swap)).astype(jnp.bfloat16)
 
 
 def solution(mesh):

time: 176 us -> 185 us (1.051); the launches traced: 174 us -> 181 us
  Pallas kernels: 104 us -> 109 us
  starting transfers between devices: 21.5 us -> 26.4 us
  other arithmetic: 5.64 us -> 3.73 us
    ppermute x16, starting transfers between devices: 21 us -> 25.9 us  [move(): return lax.ppermute(array, AXES, places.shift(**step))]
    pallas_call x3, Pallas kernels: 81.5 us -> 84 us  [contract(): pl.pallas_call(functools.partial(main_kernel, lay, stage, stages, places_...]
    pallas_call x4, Pallas kernels: 7.53 us -> 9.64 us  [pack(): pl.pallas_call(functools.partial(pack_kernel, copies), out_shape=[jax.Sha...]
  transfers between devices with their start and end apart: 18 -> 18, of which waited for: 9 -> 7; matrix products, arithmetic and copies ran while one was open for 3% -> 1% of each run, Pallas kernels for 39% -> 32%
where the time goes in v1:
time: 185 us; the launch traced here: 181 us
  Pallas kernels  109 us (59%)
  waiting for transfers between devices  37.8 us (20%)
  starting transfers between devices  26.4 us (14%)
  other arithmetic  3.73 us (2%)
  local copies, waits for them, and re-layouts  2.98 us (2%)
    pallas_call x3, Pallas kernels, contract(): pl.pallas_call(functools.partial(main_kernel, lay, stage, stages, places_...  84 us
    ppermute x16, waiting for transfers between devices, move(): return lax.ppermute(array, AXES, places.shift(**step))  33.4 us
    ppermute x16, starting transfers between devices, move(): return lax.ppermute(array, AXES, places.shift(**step))  25.9 us
    pallas_call x1, Pallas kernels, plan(): pl.pallas_call(functools.partial(plan_kernel, lay), out_shape=jax.ShapeDt...  11.3 us
    pallas_call x4, Pallas kernels, pack(): pl.pallas_call(functools.partial(pack_kernel, copies), out_shape=[jax.Sha...  9.64 us
    ppermute x1, waiting for transfers between devices, on_device(): return (own + lax.ppermute(theirs, AXES, swap)).astype(jnp.bfloat16)  4.36 us
    pallas_call x1, Pallas kernels, compress(): pl.pallas_call(functools.partial(compress_kernel, ranges, row_blocks, col...  4.03 us
  transfers between devices with their start and end apart: 18, of which 7 were waited for; matrix products, arithmetic and copies ran while one was open for 1% of the time, Pallas kernels for 32%

profile of v1, /device:TPU:0, one launch (start us, length us, event | category | flops | bytes accessed | tf_op | source)
XLA Modules:
  0.0 181.4 jit_solution(322382781293472103)
XLA Ops:
  0.5 4.0 %compress.7 = (bf16[20,128,128]{2,1,0:T(8,128)(2,1)}, bf16[10,128,128]{2,1,0:T(8,128)(2,1)}, bf16[10,128,128]{2,1,0:T(8,128)(2,1)}) custom-call(s32[32,32]{1,0:T(8,128)} %filled.3, bf16[1024,512]{1,0:T(8,128)(2,1)} %psi.1), custom_call_target="tpu_custom_call" | custom-call | tf_op jit(solution)/shard_map/compress/pallas_call | solution.py:73
  4.5 2.6 %collective-permute-start.29 = (bf16[20,128,128]{2,1,0:T(8,128)(2,1)}, bf16[20,128,128]{2,1,0:T(8,128)(2,1)S(1)}, u32[]{:S(2)}, u32[]{:S(2)}) collective-permute-start(bf16[20,128,128]{2,1,0:T(8,128)(2,1)} %get-tuple-element.216), channel_id=1, source_target_pairs={{0,16},{1,17},{2,18},{3,19},{4,20},{5,21},{6,22},{7,23},{8,24},{9,... | collective-permute-start | bytes 1966088 | tf_op jit(solution)/shard_map/ppermute | solution.py:558
  7.1 1.5 collective-permute-start.28
  8.6 1.6 collective-permute-start.27
  10.2 2.2 %collective-permute-start.31 = (bf16[10,128,128]{2,1,0:T(8,128)(2,1)}, bf16[10,128,128]{2,1,0:T(8,128)(2,1)S(1)}, u32[]{:S(2)}, u32[]{:S(2)}) collective-permute-start(bf16[10,128,128]{2,1,0:T(8,128)(2,1)} %get-tuple-element.215.refs_4_), channel_id=1, source_target_pairs={{0,6},{1,7},{2,0},{3,1},{4,2},{5,3},{6,4},{7,5},{8,14},{9,15},{10,... | collective-permute-start | bytes 983048 | tf_op jit(solution)/shard_map/ppermute | solution.py:558
  12.4 8.8 %collective-permute-done.27.refs_0_ = bf16[10,128,128]{2,1,0:T(8,128)(2,1)S(1)} collective-permute-done((bf16[10,128,128]{2,1,0:T(8,128)(2,1)}, bf16[10,128,128]{2,1,0:T(8,128)(2,1)S(1)}, u32[]{:S(2)}, u32[]{:S(2)}) %collective-permute-start.27) | collective-permute-done | bytes 327712 | tf_op jit(solution)/shard_map/ppermute | solution.py:558
  21.2 0.8 copy.7
  22.0 11.3 %plan.1.refs_0_ = s32[1786]{0:T(1024)S(1)} custom-call(s32[32,32]{1,0:T(8,128)} %filled.3, s32[4,32]{1,0:T(4,128)} %terms.1), custom_call_target="tpu_custom_call" | custom-call | tf_op jit(solution)/shard_map/plan/pallas_call | solution.py:243
  34.9 0.7 copy-done.5
  35.6 1.5 pack.16.refs_5_
  38.0 6.5 %collective-permute-start.35 = (bf16[10,128,128]{2,1,0:T(8,128)(2,1)}, bf16[10,128,128]{2,1,0:T(8,128)(2,1)S(1)}, u32[]{:S(2)}, u32[]{:S(2)}) collective-permute-start(bf16[10,128,128]{2,1,0:T(8,128)(2,1)} %get-tuple-element.224), channel_id=1, source_target_pairs={{0,2},{1,3},{2,4},{3,5},{4,6},{5,7},{6,0},{7,1},{8,10},{9,11},{10,... | collective-permute-start | bytes 983048 | tf_op jit(solution)/shard_map/ppermute | solution.py:558
  44.6 0.7 collective-permute-start.37
  45.3 6.5 %collective-permute-done.35.refs_0_ = bf16[10,128,128]{2,1,0:T(8,128)(2,1)S(1)} collective-permute-done((bf16[10,128,128]{2,1,0:T(8,128)(2,1)}, bf16[10,128,128]{2,1,0:T(8,128)(2,1)S(1)}, u32[]{:S(2)}, u32[]{:S(2)}) %collective-permute-start.35) | collective-permute-done | bytes 327712 | tf_op jit(solution)/shard_map/ppermute | solution.py:558
  51.8 0.7 copy-done.6
  52.5 2.4 %collective-permute-start.36 = (bf16[10,128,128]{2,1,0:T(8,128)(2,1)S(1)}, bf16[10,128,128]{2,1,0:T(8,128)(2,1)}, u32[]{:S(2)}, u32[]{:S(2)}) collective-permute-start(bf16[10,128,128]{2,1,0:T(8,128)(2,1)S(1)} %collective-permute-done.35.refs_0_), channel_id=1, source_target_pairs={{0,2},{1,3},{2,4},{3,5},{4,6},{5,7},{6,0},{7,1},{8,10},{9,11},{10,... | collective-permute-start | bytes 983048 | tf_op jit(solution)/shard_map/ppermute | solution.py:558
  54.9 3.0 %collective-permute-done.37.refs_2_ = bf16[10,128,128]{2,1,0:T(8,128)(2,1)} collective-permute-done((bf16[10,128,128]{2,1,0:T(8,128)(2,1)}, bf16[10,128,128]{2,1,0:T(8,128)(2,1)}, u32[]{:S(2)}, u32[]{:S(2)}) %collective-permute-start.37) | collective-permute-done | bytes 327712 | tf_op jit(solution)/shard_map/ppermute | solution.py:558
  57.9 4.1 %collective-permute-done.36.refs_1_ = bf16[10,128,128]{2,1,0:T(8,128)(2,1)} collective-permute-done((bf16[10,128,128]{2,1,0:T(8,128)(2,1)S(1)}, bf16[10,128,128]{2,1,0:T(8,128)(2,1)}, u32[]{:S(2)}, u32[]{:S(2)}) %collective-permute-start.36) | collective-permute-done | bytes 327712 | tf_op jit(solution)/shard_map/ppermute | solution.py:558
  62.0 2.4 %pack.17 = bf16[30,128,128]{2,1,0:T(8,128)(2,1)} custom-call(bf16[10,128,128]{2,1,0:T(8,128)(2,1)} %copy-done.6, bf16[10,128,128]{2,1,0:T(8,128)(2,1)} %collective-permute-done.36.refs_1_, bf16[10,128,128]{2,1,0:T(8,128)(2,1)} %collective-permute-done.37.refs_2_), custom_call_target="tpu_custom_call" | custom-call | tf_op jit(solution)/shard_map/pack/pallas_call | solution.py:475
  64.5 2.7 %pack.18 = (bf16[20,128,128]{2,1,0:T(8,128)(2,1)}, bf16[20,128,128]{2,1,0:T(8,128)(2,1)}) custom-call(bf16[20,128,128]{2,1,0:T(8,128)(2,1)S(1)} %collective-permute-done.28.refs_0_.refs_6_, bf16[30,128,128]{2,1,0:T(8,128)(2,1)} %collective-permute-done.33.refs_1_.refs_7_, bf16[30,128,128]{2,1,0:T(8,128)(2,1)S(1)} %collective-permute-done.34.refs_2_.refs_9_), custom_call_target="tpu_custom_call" | custom-call | tf_op jit(solution)/shard_map/pack/pallas_call | solution.py:475
  67.2 1.5 collective-permute-start.38
  68.7 1.5 collective-permute-start.39
  71.2 10.9 %collective-permute-done.38.refs_10_ = bf16[20,128,128]{2,1,0:T(8,128)(2,1)} collective-permute-done((bf16[20,128,128]{2,1,0:T(8,128)(2,1)}, bf16[20,128,128]{2,1,0:T(8,128)(2,1)}, u32[]{:S(2)}, u32[]{:S(2)}) %collective-permute-start.38) | collective-permute-done | bytes 655392 | tf_op jit(solution)/shard_map/ppermute | solution.py:558
  82.1 1.7 collective-permute-start.41
  83.9 1.1 collective-permute-start.40
  85.0 17.8 %early_contract.2.refs_12_ = f32[2048,512]{1,0:T(8,128)} custom-call(s32[1786]{0:T(1024)S(1)} %plan.1.refs_0_, bf16[4,4096,512]{2,1,0:T(8,128)(2,1)} %refs_1_.1, bf16[4,1024,4096]{2,1,0:T(8,128)(2,1)} %refs_2_.3, bf16[4,1024,4096]{2,1,0:T(8,128)(2,1)} %collective-permute-done.32.refs_3_, bf16[10,128,128]{2,1,0:T(8,128)(2,1)} %get-tuple-element.215.refs_4_, ...), custom_call_target="tpu_custom_call" | custom-call | flops 17179869184 | bytes 33554432 | tf_op jit(solution)/shard_map/early_contract/pallas_call | solution.py:432
  102.9 3.0 %pack.19 = (bf16[20,128,128]{2,1,0:T(8,128)(2,1)}, bf16[20,128,128]{2,1,0:T(8,128)(2,1)}) custom-call(bf16[20,128,128]{2,1,0:T(8,128)(2,1)S(1)} %collective-permute-done.28.refs_0_.refs_6_, bf16[30,128,128]{2,1,0:T(8,128)(2,1)} %collective-permute-done.40.refs_1_, bf16[30,128,128]{2,1,0:T(8,128)(2,1)} %collective-permute-done.41.refs_2_), custom_call_target="tpu_custom_call" | custom-call | tf_op jit(solution)/shard_map/pack/pallas_call | solution.py:475
  105.9 1.2 collective-permute-start.42
  107.5 19.1 %early_contract.3 = f32[2048,512]{1,0:T(8,128)} custom-call(s32[1786]{0:T(1024)S(1)} %plan.1.refs_0_, bf16[4,4096,512]{2,1,0:T(8,128)(2,1)} %refs_1_.1, bf16[4,1024,4096]{2,1,0:T(8,128)(2,1)} %refs_2_.3, bf16[4,1024,4096]{2,1,0:T(8,128)(2,1)} %collective-permute-done.32.refs_3_, bf16[10,128,128]{2,1,0:T(8,128)(2,1)} %get-tuple-element.215.refs_4_, ...), custom_call_target="tpu_custom_call" | custom-call | flops 17179869184 | bytes 33554432 | tf_op jit(solution)/shard_map/early_contract/pallas_call | solution.py:432
  126.6 47.4 %conditional.1 = ((f32[1024,512]{1,0:T(8,128)}, f32[1024,512]{1,0:T(8,128)})) conditional(s32[]{:T(128)} %clamp.3, (s32[1786]{0:T(1024)S(1)}, bf16[4,4096,512]{2,1,0:T(8,128)(2,1)}, bf16[4,1024,4096]{2,1,0:T(8,128)(2,1)}, bf16[4,1024,4096]{2,1,0:T(8,128)(2,1)}, bf16[10,128,128]{2,1,0:T(8,128)(2,1)}, ...), branch_computations={%region_2.3_spmd, %region_3.4_spmd, %region_4.5_spmd} | conditional | flops 17179869184 | bytes 62972664 | solution.py:619
  126.7 47.1 %late_contract.3 = (f32[1024,512]{1,0:T(8,128)}, f32[1024,512]{1,0:T(8,128)}) custom-call(s32[1786]{0:T(1024)S(1)} %get-tuple-element.127.refs_0_, bf16[4,4096,512]{2,1,0:T(8,128)(2,1)} %get-tuple-element.128.refs_1_, bf16[4,1024,4096]{2,1,0:T(8,128)(2,1)} %get-tuple-element.129.refs_2_, bf16[4,1024,4096]{2,1,0:T(8,128)(2,1)} %get-tuple-element.130.refs_3_, ...), custom_call_target="tpu_custom_call" | custom-call | flops 17179869184 | bytes 33554432 | tf_op jit(solution)/shard_map/cond/branch_0_fun/late_contract/pallas_call | solution.py:432
  174.1 4.4 %collective-permute-done.44 = f32[1024,512]{1,0:T(8,128)S(1)} collective-permute-done((f32[1024,512]{1,0:T(8,128)}, f32[1024,512]{1,0:T(8,128)S(1)}, u32[]{:S(2)}, u32[]{:S(2)}) %collective-permute-start.44) | collective-permute-done | bytes 2097184 | tf_op jit(solution)/shard_map/ppermute | solution.py:620
  178.5 2.9 %add_convert_fusion = bf16[1024,512]{1,0:T(8,128)(2,1)} fusion(f32[1024,512]{1,0:T(8,128)} %get-tuple-element.234, f32[1024,512]{1,0:T(8,128)S(1)} %collective-permute-done.44), kind=kLoop, calls=%fused_computation | loop fusion | flops 1048576 | bytes 5242880 | tf_op jit(solution)/shard_map/convert_element_type | solution.py:620
  (29 shorter events, 3.5 us)
Async XLA Ops:
  0.0 85.0 %collective-permute-start.32 = (bf16[4,1024,4096]{2,1,0:T(8,128)(2,1)}, bf16[4,1024,4096]{2,1,0:T(8,128)(2,1)}, u32[]{:S(2)}, u32[]{:S(2)}) collective-permute-start(bf16[4,1024,4096]{2,1,0:T(8,128)(2,1)} %refs_2_.3), channel_id=1, source_target_pairs={{0,8},{1,9},{2,10},{3,11},{4,12},{5,13},{6,14},{7,15},{8,0},{9,1},... | collective-permute-start | bytes 100663304 | tf_op jit(solution)/shard_map/ppermute | solution.py:577
  4.5 29.7 %collective-permute-start.29 = (bf16[20,128,128]{2,1,0:T(8,128)(2,1)}, bf16[20,128,128]{2,1,0:T(8,128)(2,1)S(1)}, u32[]{:S(2)}, u32[]{:S(2)}) collective-permute-start(bf16[20,128,128]{2,1,0:T(8,128)(2,1)} %get-tuple-element.216), channel_id=1, source_target_pairs={{0,16},{1,17},{2,18},{3,19},{4,20},{5,21},{6,22},{7,23},{8,24},{9,... | collective-permute-start | bytes 1966088 | tf_op jit(solution)/shard_map/ppermute | solution.py:558
  7.1 27.1 %collective-permute-start.28 = (bf16[20,128,128]{2,1,0:T(8,128)(2,1)}, bf16[20,128,128]{2,1,0:T(8,128)(2,1)S(1)}, u32[]{:S(2)}, u32[]{:S(2)}) collective-permute-start(bf16[20,128,128]{2,1,0:T(8,128)(2,1)} %get-tuple-element.216), channel_id=1, source_target_pairs={{0,1},{1,0},{2,3},{3,2},{4,5},{5,4},{6,7},{7,6},{8,9},{9,8},{10,11... | collective-permute-start | bytes 1966088 | tf_op jit(solution)/shard_map/ppermute | solution.py:558
  8.6 12.6 %collective-permute-start.27 = (bf16[10,128,128]{2,1,0:T(8,128)(2,1)}, bf16[10,128,128]{2,1,0:T(8,128)(2,1)S(1)}, u32[]{:S(2)}, u32[]{:S(2)}) collective-permute-start(bf16[10,128,128]{2,1,0:T(8,128)(2,1)} %get-tuple-element.215.refs_4_), channel_id=1, source_target_pairs={{0,2},{1,3},{2,4},{3,5},{4,6},{5,7},{6,0},{7,1},{8,10},{9,11},{10,... | collective-permute-start | bytes 983048 | tf_op jit(solution)/shard_map/ppermute | solution.py:558
  10.2 24.0 %collective-permute-start.31 = (bf16[10,128,128]{2,1,0:T(8,128)(2,1)}, bf16[10,128,128]{2,1,0:T(8,128)(2,1)S(1)}, u32[]{:S(2)}, u32[]{:S(2)}) collective-permute-start(bf16[10,128,128]{2,1,0:T(8,128)(2,1)} %get-tuple-element.215.refs_4_), channel_id=1, source_target_pairs={{0,6},{1,7},{2,0},{3,1},{4,2},{5,3},{6,4},{7,5},{8,14},{9,15},{10,... | collective-permute-start | bytes 983048 | tf_op jit(solution)/shard_map/ppermute | solution.py:558
  21.2 13.1 %copy-start.3 = (bf16[10,128,128]{2,1,0:T(8,128)(2,1)}, bf16[10,128,128]{2,1,0:T(8,128)(2,1)S(1)}, u32[]{:S(2)}) copy-start(bf16[10,128,128]{2,1,0:T(8,128)(2,1)S(1)} %collective-permute-done.27.refs_0_) | copy-start | bytes 983044
  21.2 13.1 %collective-permute-start.30 = (bf16[10,128,128]{2,1,0:T(8,128)(2,1)S(1)}, bf16[10,128,128]{2,1,0:T(8,128)(2,1)S(1)}, u32[]{:S(2)}, u32[]{:S(2)}) collective-permute-start(bf16[10,128,128]{2,1,0:T(8,128)(2,1)S(1)} %collective-permute-done.27.refs_0_), channel_id=1, source_target_pairs={{0,2},{1,3},{2,4},{3,5},{4,6},{5,7},{6,0},{7,1},{8,10},{9,11},{10,... | collective-permute-start | bytes 983048 | tf_op jit(solution)/shard_map/ppermute | solution.py:558
  34.2 0.7 copy-start.4
  34.9 0.7 copy-start.5
  37.2 27.3 %collective-permute-start.34 = (bf16[30,128,128]{2,1,0:T(8,128)(2,1)S(1)}, bf16[30,128,128]{2,1,0:T(8,128)(2,1)S(1)}, u32[]{:S(2)}, u32[]{:S(2)}) collective-permute-start(bf16[30,128,128]{2,1,0:T(8,128)(2,1)S(1)} %pack.16.refs_5_), channel_id=1, source_target_pairs={{0,16},{1,17},{2,18},{3,19},{4,20},{5,21},{6,22},{7,23},{8,24},{9,... | collective-permute-start | bytes 2949128 | tf_op jit(solution)/shard_map/ppermute | solution.py:558
  37.8 26.7 %collective-permute-start.33 = (bf16[30,128,128]{2,1,0:T(8,128)(2,1)S(1)}, bf16[30,128,128]{2,1,0:T(8,128)(2,1)}, u32[]{:S(2)}, u32[]{:S(2)}) collective-permute-start(bf16[30,128,128]{2,1,0:T(8,128)(2,1)S(1)} %pack.16.refs_5_), channel_id=1, source_target_pairs={{0,1},{1,0},{2,3},{3,2},{4,5},{5,4},{6,7},{7,6},{8,9},{9,8},{10,11... | collective-permute-start | bytes 2949128 | tf_op jit(solution)/shard_map/ppermute | solution.py:558
  38.0 13.8 %collective-permute-start.35 = (bf16[10,128,128]{2,1,0:T(8,128)(2,1)}, bf16[10,128,128]{2,1,0:T(8,128)(2,1)S(1)}, u32[]{:S(2)}, u32[]{:S(2)}) collective-permute-start(bf16[10,128,128]{2,1,0:T(8,128)(2,1)} %get-tuple-element.224), channel_id=1, source_target_pairs={{0,2},{1,3},{2,4},{3,5},{4,6},{5,7},{6,0},{7,1},{8,10},{9,11},{10,... | collective-permute-start | bytes 983048 | tf_op jit(solution)/shard_map/ppermute | solution.py:558
  44.6 13.3 %collective-permute-start.37 = (bf16[10,128,128]{2,1,0:T(8,128)(2,1)}, bf16[10,128,128]{2,1,0:T(8,128)(2,1)}, u32[]{:S(2)}, u32[]{:S(2)}) collective-permute-start(bf16[10,128,128]{2,1,0:T(8,128)(2,1)} %get-tuple-element.224), channel_id=1, source_target_pairs={{0,6},{1,7},{2,0},{3,1},{4,2},{5,3},{6,4},{7,5},{8,14},{9,15},{10,... | collective-permute-start | bytes 983048 | tf_op jit(solution)/shard_map/ppermute | solution.py:558
  51.8 0.7 copy-start.6
  52.5 9.5 %collective-permute-start.36 = (bf16[10,128,128]{2,1,0:T(8,128)(2,1)S(1)}, bf16[10,128,128]{2,1,0:T(8,128)(2,1)}, u32[]{:S(2)}, u32[]{:S(2)}) collective-permute-start(bf16[10,128,128]{2,1,0:T(8,128)(2,1)S(1)} %collective-permute-done.35.refs_0_), channel_id=1, source_target_pairs={{0,2},{1,3},{2,4},{3,5},{4,6},{5,7},{6,0},{7,1},{8,10},{9,11},{10,... | collective-permute-start | bytes 983048 | tf_op jit(solution)/shard_map/ppermute | solution.py:558
  67.2 15.0 %collective-permute-start.38 = (bf16[20,128,128]{2,1,0:T(8,128)(2,1)}, bf16[20,128,128]{2,1,0:T(8,128)(2,1)}, u32[]{:S(2)}, u32[]{:S(2)}) collective-permute-start(bf16[20,128,128]{2,1,0:T(8,128)(2,1)} %get-tuple-element.226), channel_id=1, source_target_pairs={{0,16},{1,17},{2,18},{3,19},{4,20},{5,21},{6,22},{7,23},{8,24},{9,... | collective-permute-start | bytes 1966088 | tf_op jit(solution)/shard_map/ppermute | solution.py:558
  68.7 13.5 %collective-permute-start.39 = (bf16[20,128,128]{2,1,0:T(8,128)(2,1)}, bf16[20,128,128]{2,1,0:T(8,128)(2,1)}, u32[]{:S(2)}, u32[]{:S(2)}) collective-permute-start(bf16[20,128,128]{2,1,0:T(8,128)(2,1)} %get-tuple-element.227), channel_id=1, source_target_pairs={{0,1},{1,0},{2,3},{3,2},{4,5},{5,4},{6,7},{7,6},{8,9},{9,8},{10,11... | collective-permute-start | bytes 1966088 | tf_op jit(solution)/shard_map/ppermute | solution.py:558
  82.1 20.7 %collective-permute-start.41 = (bf16[30,128,128]{2,1,0:T(8,128)(2,1)}, bf16[30,128,128]{2,1,0:T(8,128)(2,1)}, u32[]{:S(2)}, u32[]{:S(2)}) collective-permute-start(bf16[30,128,128]{2,1,0:T(8,128)(2,1)} %pack.17), channel_id=1, source_target_pairs={{0,16},{1,17},{2,18},{3,19},{4,20},{5,21},{6,22},{7,23},{8,24},{9,... | collective-permute-start | bytes 2949128 | tf_op jit(solution)/shard_map/ppermute | solution.py:558
  83.9 19.0 %collective-permute-start.40 = (bf16[30,128,128]{2,1,0:T(8,128)(2,1)}, bf16[30,128,128]{2,1,0:T(8,128)(2,1)}, u32[]{:S(2)}, u32[]{:S(2)}) collective-permute-start(bf16[30,128,128]{2,1,0:T(8,128)(2,1)} %pack.17), channel_id=1, source_target_pairs={{0,1},{1,0},{2,3},{3,2},{4,5},{5,4},{6,7},{7,6},{8,9},{9,8},{10,11... | collective-permute-start | bytes 2949128 | tf_op jit(solution)/shard_map/ppermute | solution.py:558
  105.9 20.7 %collective-permute-start.42 = (bf16[20,128,128]{2,1,0:T(8,128)(2,1)}, bf16[20,128,128]{2,1,0:T(8,128)(2,1)}, u32[]{:S(2)}, u32[]{:S(2)}) collective-permute-start(bf16[20,128,128]{2,1,0:T(8,128)(2,1)} %get-tuple-element.231), channel_id=1, source_target_pairs={{0,16},{1,17},{2,18},{3,19},{4,20},{5,21},{6,22},{7,23},{8,24},{9,... | collective-permute-start | bytes 1966088 | tf_op jit(solution)/shard_map/ppermute | solution.py:558
  107.1 19.6 %copy-start.1 = (s32[32,32]{1,0:T(8,128)S(1)}, s32[32,32]{1,0:T(8,128)}, u32[]{:S(2)}) copy-start(s32[32,32]{1,0:T(8,128)} %filled.3) | copy-start | bytes 12292
  107.1 19.6 %collective-permute-start.43 = (bf16[20,128,128]{2,1,0:T(8,128)(2,1)}, bf16[20,128,128]{2,1,0:T(8,128)(2,1)}, u32[]{:S(2)}, u32[]{:S(2)}) collective-permute-start(bf16[20,128,128]{2,1,0:T(8,128)(2,1)} %get-tuple-element.232), channel_id=1, source_target_pairs={{0,1},{1,0},{2,3},{3,2},{4,5},{5,4},{6,7},{7,6},{8,9},{9,8},{10,11... | collective-permute-start | bytes 1966088 | tf_op jit(solution)/shard_map/ppermute | solution.py:558
  174.0 4.4 %collective-permute-start.44 = (f32[1024,512]{1,0:T(8,128)}, f32[1024,512]{1,0:T(8,128)S(1)}, u32[]{:S(2)}, u32[]{:S(2)}) collective-permute-start(f32[1024,512]{1,0:T(8,128)} %get-tuple-element.235), channel_id=1, source_target_pairs={{0,8},{1,9},{2,10},{3,11},{4,12},{5,13},{6,14},{7,15},{8,0},{9,1},... | collective-permute-start | bytes 6291464 | tf_op jit(solution)/shard_map/ppermute | solution.py:620

commit v2 on v1

--- a/solution.py
+++ b/solution.py
@@ -154,7 +154,6 @@
         dy = (y_me - y + py) % py
         k_block = (y * CORES + core) * lay.row_blocks + kb
         n = jnp.int32(0)
-        most = jnp.int32(0)
         for dev in range(lay.places.cols):
             dz = (z_me - dev // px + pz) % pz
             dx = (x_me - dev % px + px) % px
@@ -171,7 +170,6 @@
                 n = n + here
                 slot = slot + here
             used[dev] = slot
-            most = jnp.maximum(most, slot)
 
         def pad(i, carry):
             spots[q * lay.stride + i] = 0
@@ -180,7 +178,7 @@
 
         lax.fori_loop(n, lay.stride, pad, 0)
         counts[q] = n
-        early = jnp.where(most <= lay.chunks[0], 1, 0)
+        early = jnp.where(y == y_me, 1, 0)
         ready[q] = early
         for t in range(lay.terms):
             n_ready = n_ready + jnp.where((terms[t, k_block] != 0) & (n > 0), early, 0)
@@ -540,13 +538,20 @@
         }
         return [*self.rest_over_y.values(), *self.rest_over_x.values()]
 
+    def own_y(self):
+        z, w = self.places.z, self.wide
+        got = [(0, self.part, 0, w), (1, self.q, 0, (z - 1) * w)]
+        for i in range(len(self.x_own)):
+            got.append(((i + 1) * z, self.x_own[i], self.first, w))
+            got.append(((i + 1) * z + 1, self.x_line[i], 0, (z - 1) * w))
+        return got
+
     def arrays(self):
         x, z, w = self.places.x, self.places.z, self.wide
-        got = [(0, self.part, 0, w), (1, self.q, 0, (z - 1) * w)]
-        for own, line, step in ((self.x_own, self.x_line, z), (self.y_own, self.y_line, x * z)):
-            for i in range(len(own)):
-                got.append(((i + 1) * step, own[i], self.first, w))
-                got.append(((i + 1) * step + 1, line[i], 0, (z - 1) * w))
+        got = self.own_y()
+        for i in range(len(self.y_own)):
+            got.append(((i + 1) * x * z, self.y_own[i], self.first, w))
+            got.append(((i + 1) * x * z + 1, self.y_line[i], 0, (z - 1) * w))
         for (dy, dx), array in self.rest_over_y.items():
             got.append(((dy * x + dx) * z, array, 0, array.shape[0]))
         for (dy, dx), array in self.rest_over_x.items():
@@ -583,17 +588,14 @@
     one.q, table, most = lax.optimization_barrier((one.q, table, most))
     one.over_xy()
     two.over_z(one.q)
-    two.pack_z()
-    one.pack_rest(two.q)
-    diagonal = one.rest()
-    first = one.arrays()
-    two.q = after(two.q, *diagonal)
+    two.pack_z(*one.x_line, *one.y_line)
     two.over_xy()
-    early = contract(lay, 0, 2, table, after(right_env, two.q), left_env, sib, [first])
-    gone = two.pack_rest(early)
+    gone = [one.pack_rest(*two.x_line, *two.y_line), two.pack_rest()]
+    first, second = one.own_y(), two.own_y()
+    early = contract(lay, 0, 1, table, after(right_env, *gone), left_env, sib, [first, second])
+    one.rest()
     two.rest()
-    early = contract(lay, 1, 2, table, after(right_env, gone), left_env, sib, [first], early)
-    second = two.arrays()
+    first, second = one.arrays(), two.arrays()
 
     def finish(extra, _):
         low, parts = base, [first, second]
@@ -613,7 +615,7 @@
             more.rest()
             parts.append(more.arrays())
             low += wide
-        return contract(lay, 2, 2, table, right_env, left_env, sib, parts, early)
+        return contract(lay, 1, 1, table, right_env, left_env, sib, parts, early)
 
     levels = jnp.where(most > base, 1, 0) + jnp.where(most > base + chunks[2], 1, 0)
     own, theirs = lax.switch(levels, [functools.partial(finish, extra) for extra in range(3)], 0)

time: 185 us -> 185 us (level); the launches traced: 181 us -> 184 us
  waiting for transfers between devices: 37.8 us -> 44.8 us
  Pallas kernels: 109 us -> 106 us
    ppermute x16, waiting for transfers between devices: 33.4 us -> 40.4 us  [move(): return lax.ppermute(array, AXES, places.shift(**step))]
    pallas_call x3 -> x2, Pallas kernels: 84 us -> 80.6 us  [contract(): pl.pallas_call(functools.partial(main_kernel, lay, stage, stages, places_...]
  transfers between devices with their start and end apart: 18 -> 18, of which waited for: 7 -> 10; matrix products, arithmetic and copies ran while one was open for 1% -> 1% of each run, Pallas kernels for 32% -> 33%
where the time goes in v2:
time: 185 us; the launch traced here: 184 us
  Pallas kernels  106 us (57%)
  waiting for transfers between devices  44.8 us (24%)
  starting transfers between devices  25.8 us (14%)
  other arithmetic  3.73 us (2%)
  local copies, waits for them, and re-layouts  2.27 us (1%)
    pallas_call x2, Pallas kernels, contract(): pl.pallas_call(functools.partial(main_kernel, lay, stage, stages, places_...  80.6 us
    ppermute x16, waiting for transfers between devices, move(): return lax.ppermute(array, AXES, places.shift(**step))  40.4 us
    ppermute x16, starting transfers between devices, move(): return lax.ppermute(array, AXES, places.shift(**step))  25.3 us
    pallas_call x1, Pallas kernels, plan(): pl.pallas_call(functools.partial(plan_kernel, lay), out_shape=jax.ShapeDt...  11.3 us
    pallas_call x4, Pallas kernels, pack(): pl.pallas_call(functools.partial(pack_kernel, copies), out_shape=[jax.Sha...  9.64 us
    ppermute x1, waiting for transfers between devices, on_device(): return (own + lax.ppermute(theirs, AXES, swap)).astype(jnp.bfloat16)  4.36 us
    pallas_call x1, Pallas kernels, compress(): pl.pallas_call(functools.partial(compress_kernel, ranges, row_blocks, col...  4.04 us
  transfers between devices with their start and end apart: 18, of which 10 were waited for; matrix products, arithmetic and copies ran while one was open for 1% of the time, Pallas kernels for 33%

profile of v2, /device:TPU:0, one launch (start us, length us, event | category | flops | bytes accessed | tf_op | source)
XLA Modules:
  0.0 183.8 jit_solution(11409986949192997839)
XLA Ops:
  0.5 4.0 %compress.7 = (bf16[20,128,128]{2,1,0:T(8,128)(2,1)}, bf16[10,128,128]{2,1,0:T(8,128)(2,1)}, bf16[10,128,128]{2,1,0:T(8,128)(2,1)}) custom-call(s32[32,32]{1,0:T(8,128)} %filled.3, bf16[1024,512]{1,0:T(8,128)(2,1)} %psi.1), custom_call_target="tpu_custom_call" | custom-call | tf_op jit(solution)/shard_map/compress/pallas_call | solution.py:73
  4.5 2.6 %collective-permute-start.29 = (bf16[20,128,128]{2,1,0:T(8,128)(2,1)}, bf16[20,128,128]{2,1,0:T(8,128)(2,1)S(1)}, u32[]{:S(2)}, u32[]{:S(2)}) collective-permute-start(bf16[20,128,128]{2,1,0:T(8,128)(2,1)} %get-tuple-element.216), channel_id=1, source_target_pairs={{0,16},{1,17},{2,18},{3,19},{4,20},{5,21},{6,22},{7,23},{8,24},{9,... | collective-permute-start | bytes 1966088 | tf_op jit(solution)/shard_map/ppermute | solution.py:563
  7.1 1.5 collective-permute-start.28
  8.6 1.6 collective-permute-start.27
  10.2 2.2 %collective-permute-start.31 = (bf16[10,128,128]{2,1,0:T(8,128)(2,1)}, bf16[10,128,128]{2,1,0:T(8,128)(2,1)S(1)}, u32[]{:S(2)}, u32[]{:S(2)}) collective-permute-start(bf16[10,128,128]{2,1,0:T(8,128)(2,1)} %get-tuple-element.215.refs_4_), channel_id=1, source_target_pairs={{0,6},{1,7},{2,0},{3,1},{4,2},{5,3},{6,4},{7,5},{8,14},{9,15},{10,... | collective-permute-start | bytes 983048 | tf_op jit(solution)/shard_map/ppermute | solution.py:563
  12.4 8.8 %collective-permute-done.27.refs_0_ = bf16[10,128,128]{2,1,0:T(8,128)(2,1)S(1)} collective-permute-done((bf16[10,128,128]{2,1,0:T(8,128)(2,1)}, bf16[10,128,128]{2,1,0:T(8,128)(2,1)S(1)}, u32[]{:S(2)}, u32[]{:S(2)}) %collective-permute-start.27) | collective-permute-done | bytes 327712 | tf_op jit(solution)/shard_map/ppermute | solution.py:563
  21.2 0.8 copy.7
  22.0 11.3 %plan.1.refs_0_ = s32[1786]{0:T(1024)S(1)} custom-call(s32[32,32]{1,0:T(8,128)} %filled.3, s32[4,32]{1,0:T(4,128)} %terms.1), custom_call_target="tpu_custom_call" | custom-call | tf_op jit(solution)/shard_map/plan/pallas_call | solution.py:241
  34.3 0.7 copy-done.4
  34.9 0.7 copy-done.5
  35.7 1.5 pack.16.refs_5_
  38.0 5.9 %collective-permute-start.35 = (bf16[10,128,128]{2,1,0:T(8,128)(2,1)}, bf16[10,128,128]{2,1,0:T(8,128)(2,1)S(1)}, u32[]{:S(2)}, u32[]{:S(2)}) collective-permute-start(bf16[10,128,128]{2,1,0:T(8,128)(2,1)} %get-tuple-element.224.refs_8_), channel_id=1, source_target_pairs={{0,2},{1,3},{2,4},{3,5},{4,6},{5,7},{6,0},{7,1},{8,10},{9,11},{10,... | collective-permute-start | bytes 983048 | tf_op jit(solution)/shard_map/ppermute | solution.py:563
  44.0 1.2 collective-permute-start.37
  45.2 6.6 %collective-permute-done.35.refs_0_ = bf16[10,128,128]{2,1,0:T(8,128)(2,1)S(1)} collective-permute-done((bf16[10,128,128]{2,1,0:T(8,128)(2,1)}, bf16[10,128,128]{2,1,0:T(8,128)(2,1)S(1)}, u32[]{:S(2)}, u32[]{:S(2)}) %collective-permute-start.35) | collective-permute-done | bytes 327712 | tf_op jit(solution)/shard_map/ppermute | solution.py:563
  51.8 2.4 %collective-permute-start.36 = (bf16[10,128,128]{2,1,0:T(8,128)(2,1)S(1)}, bf16[10,128,128]{2,1,0:T(8,128)(2,1)}, u32[]{:S(2)}, u32[]{:S(2)}) collective-permute-start(bf16[10,128,128]{2,1,0:T(8,128)(2,1)S(1)} %collective-permute-done.35.refs_0_), channel_id=1, source_target_pairs={{0,2},{1,3},{2,4},{3,5},{4,6},{5,7},{6,0},{7,1},{8,10},{9,11},{10,... | collective-permute-start | bytes 983048 | tf_op jit(solution)/shard_map/ppermute | solution.py:563
  54.2 3.8 %collective-permute-done.37.refs_2_ = bf16[10,128,128]{2,1,0:T(8,128)(2,1)S(1)} collective-permute-done((bf16[10,128,128]{2,1,0:T(8,128)(2,1)}, bf16[10,128,128]{2,1,0:T(8,128)(2,1)S(1)}, u32[]{:S(2)}, u32[]{:S(2)}) %collective-permute-start.37) | collective-permute-done | bytes 327712 | tf_op jit(solution)/shard_map/ppermute | solution.py:563
  58.0 1.2 collective-permute-done.34.refs_2_
  59.3 2.7 %collective-permute-done.36.refs_1_ = bf16[10,128,128]{2,1,0:T(8,128)(2,1)} collective-permute-done((bf16[10,128,128]{2,1,0:T(8,128)(2,1)S(1)}, bf16[10,128,128]{2,1,0:T(8,128)(2,1)}, u32[]{:S(2)}, u32[]{:S(2)}) %collective-permute-start.36) | collective-permute-done | bytes 327712 | tf_op jit(solution)/shard_map/ppermute | solution.py:563
  62.0 2.4 %pack.17.refs_9_ = bf16[30,128,128]{2,1,0:T(8,128)(2,1)} custom-call(bf16[10,128,128]{2,1,0:T(8,128)(2,1)} %copy-done.6, bf16[10,128,128]{2,1,0:T(8,128)(2,1)} %collective-permute-done.36.refs_1_, bf16[10,128,128]{2,1,0:T(8,128)(2,1)} %copy-done.7), custom_call_target="tpu_custom_call" | custom-call | tf_op jit(solution)/shard_map/pack/pallas_call | solution.py:473
  64.5 1.4 collective-permute-start.39
  65.9 1.4 collective-permute-start.38
  68.5 16.2 %collective-permute-done.39.refs_2_ = bf16[30,128,128]{2,1,0:T(8,128)(2,1)} collective-permute-done((bf16[30,128,128]{2,1,0:T(8,128)(2,1)}, bf16[30,128,128]{2,1,0:T(8,128)(2,1)}, u32[]{:S(2)}, u32[]{:S(2)}) %collective-permute-start.39) | collective-permute-done | bytes 983072 | tf_op jit(solution)/shard_map/ppermute | solution.py:563
  84.6 0.9 collective-permute-done.38.refs_1_.refs_11_
  85.5 2.7 %pack.18 = (bf16[20,128,128]{2,1,0:T(8,128)(2,1)}, bf16[20,128,128]{2,1,0:T(8,128)(2,1)}) custom-call(bf16[20,128,128]{2,1,0:T(8,128)(2,1)S(1)} %collective-permute-done.28.refs_0_.refs_6_.refs_10_, bf16[30,128,128]{2,1,0:T(8,128)(2,1)S(1)} %collective-permute-done.33.refs_1_.refs_7_, bf16[30,128,128]{2,1,0:T(8,128)(2,1)} %collective-permute-done.34.refs_2_), custom_call_target="tpu_custom_call" | custom-call | tf_op jit(solution)/shard_map/pack/pallas_call | solution.py:473
  88.3 1.5 collective-permute-start.41
  90.2 3.0 %pack.19 = (bf16[20,128,128]{2,1,0:T(8,128)(2,1)}, bf16[20,128,128]{2,1,0:T(8,128)(2,1)}) custom-call(bf16[20,128,128]{2,1,0:T(8,128)(2,1)S(1)} %collective-permute-done.28.refs_0_.refs_6_.refs_10_, bf16[30,128,128]{2,1,0:T(8,128)(2,1)} %collective-permute-done.38.refs_1_.refs_11_, bf16[30,128,128]{2,1,0:T(8,128)(2,1)} %collective-permute-done.39.refs_2_), custom_call_target="tpu_custom_call" | custom-call | tf_op jit(solution)/shard_map/pack/pallas_call | solution.py:473
  93.2 1.6 collective-permute-start.42
  95.5 35.4 %early_contract.1 = f32[2048,512]{1,0:T(8,128)} custom-call(s32[1786]{0:T(1024)S(1)} %plan.1.refs_0_, bf16[4,4096,512]{2,1,0:T(8,128)(2,1)} %refs_1_, bf16[4,1024,4096]{2,1,0:T(8,128)(2,1)} %refs_2_.1, bf16[4,1024,4096]{2,1,0:T(8,128)(2,1)} %collective-permute-done.32.refs_3_, bf16[10,128,128]{2,1,0:T(8,128)(2,1)} %get-tuple-element.215.refs_4_, ...), custom_call_target="tpu_custom_call" | custom-call | flops 17179869184 | bytes 33554432 | tf_op jit(solution)/shard_map/early_contract/pallas_call | solution.py:430
  130.9 45.5 %conditional.1 = ((f32[1024,512]{1,0:T(8,128)}, f32[1024,512]{1,0:T(8,128)})) conditional(s32[]{:T(128)} %clamp.3, (s32[1786]{0:T(1024)S(1)}, bf16[4,4096,512]{2,1,0:T(8,128)(2,1)}, bf16[4,1024,4096]{2,1,0:T(8,128)(2,1)}, bf16[4,1024,4096]{2,1,0:T(8,128)(2,1)}, bf16[10,128,128]{2,1,0:T(8,128)(2,1)}, ...), branch_computations={%region_2.3_spmd, %region_3.4_spmd, %region_4.5_spmd} | conditional | flops 17179869184 | bytes 62972664 | solution.py:621
  131.0 45.2 %late_contract.3 = (f32[1024,512]{1,0:T(8,128)}, f32[1024,512]{1,0:T(8,128)}) custom-call(s32[1786]{0:T(1024)S(1)} %get-tuple-element.127.refs_0_, bf16[4,4096,512]{2,1,0:T(8,128)(2,1)} %get-tuple-element.128.refs_1_, bf16[4,1024,4096]{2,1,0:T(8,128)(2,1)} %get-tuple-element.129.refs_2_, bf16[4,1024,4096]{2,1,0:T(8,128)(2,1)} %get-tuple-element.130.refs_3_, ...), custom_call_target="tpu_custom_call" | custom-call | flops 17179869184 | bytes 33554432 | tf_op jit(solution)/shard_map/cond/branch_0_fun/late_contract/pallas_call | solution.py:430
  176.5 4.4 %collective-permute-done.44 = f32[1024,512]{1,0:T(8,128)S(1)} collective-permute-done((f32[1024,512]{1,0:T(8,128)}, f32[1024,512]{1,0:T(8,128)S(1)}, u32[]{:S(2)}, u32[]{:S(2)}) %collective-permute-start.44) | collective-permute-done | bytes 2097184 | tf_op jit(solution)/shard_map/ppermute | solution.py:622
  180.8 2.9 %add_convert_fusion = bf16[1024,512]{1,0:T(8,128)(2,1)} fusion(f32[1024,512]{1,0:T(8,128)} %get-tuple-element.234, f32[1024,512]{1,0:T(8,128)S(1)} %collective-permute-done.44), kind=kLoop, calls=%fused_computation | loop fusion | flops 1048576 | bytes 5242880 | tf_op jit(solution)/shard_map/convert_element_type | solution.py:622
  (30 shorter events, 3.7 us)
Async XLA Ops:
  0.0 95.4 %collective-permute-start.32 = (bf16[4,1024,4096]{2,1,0:T(8,128)(2,1)}, bf16[4,1024,4096]{2,1,0:T(8,128)(2,1)}, u32[]{:S(2)}, u32[]{:S(2)}) collective-permute-start(bf16[4,1024,4096]{2,1,0:T(8,128)(2,1)} %refs_2_.1), channel_id=1, source_target_pairs={{0,8},{1,9},{2,10},{3,11},{4,12},{5,13},{6,14},{7,15},{8,0},{9,1},... | collective-permute-start | bytes 100663304 | tf_op jit(solution)/shard_map/ppermute | solution.py:582
  4.5 29.7 %collective-permute-start.29 = (bf16[20,128,128]{2,1,0:T(8,128)(2,1)}, bf16[20,128,128]{2,1,0:T(8,128)(2,1)S(1)}, u32[]{:S(2)}, u32[]{:S(2)}) collective-permute-start(bf16[20,128,128]{2,1,0:T(8,128)(2,1)} %get-tuple-element.216), channel_id=1, source_target_pairs={{0,16},{1,17},{2,18},{3,19},{4,20},{5,21},{6,22},{7,23},{8,24},{9,... | collective-permute-start | bytes 1966088 | tf_op jit(solution)/shard_map/ppermute | solution.py:563
  7.1 27.2 %collective-permute-start.28 = (bf16[20,128,128]{2,1,0:T(8,128)(2,1)}, bf16[20,128,128]{2,1,0:T(8,128)(2,1)S(1)}, u32[]{:S(2)}, u32[]{:S(2)}) collective-permute-start(bf16[20,128,128]{2,1,0:T(8,128)(2,1)} %get-tuple-element.216), channel_id=1, source_target_pairs={{0,1},{1,0},{2,3},{3,2},{4,5},{5,4},{6,7},{7,6},{8,9},{9,8},{10,11... | collective-permute-start | bytes 1966088 | tf_op jit(solution)/shard_map/ppermute | solution.py:563
  8.6 12.6 %collective-permute-start.27 = (bf16[10,128,128]{2,1,0:T(8,128)(2,1)}, bf16[10,128,128]{2,1,0:T(8,128)(2,1)S(1)}, u32[]{:S(2)}, u32[]{:S(2)}) collective-permute-start(bf16[10,128,128]{2,1,0:T(8,128)(2,1)} %get-tuple-element.215.refs_4_), channel_id=1, source_target_pairs={{0,2},{1,3},{2,4},{3,5},{4,6},{5,7},{6,0},{7,1},{8,10},{9,11},{10,... | collective-permute-start | bytes 983048 | tf_op jit(solution)/shard_map/ppermute | solution.py:563
  10.2 24.1 %collective-permute-start.31 = (bf16[10,128,128]{2,1,0:T(8,128)(2,1)}, bf16[10,128,128]{2,1,0:T(8,128)(2,1)S(1)}, u32[]{:S(2)}, u32[]{:S(2)}) collective-permute-start(bf16[10,128,128]{2,1,0:T(8,128)(2,1)} %get-tuple-element.215.refs_4_), channel_id=1, source_target_pairs={{0,6},{1,7},{2,0},{3,1},{4,2},{5,3},{6,4},{7,5},{8,14},{9,15},{10,... | collective-permute-start | bytes 983048 | tf_op jit(solution)/shard_map/ppermute | solution.py:563
  21.2 13.1 %copy-start.3 = (bf16[10,128,128]{2,1,0:T(8,128)(2,1)}, bf16[10,128,128]{2,1,0:T(8,128)(2,1)S(1)}, u32[]{:S(2)}) copy-start(bf16[10,128,128]{2,1,0:T(8,128)(2,1)S(1)} %collective-permute-done.27.refs_0_) | copy-start | bytes 983044
  21.2 13.1 %collective-permute-start.30 = (bf16[10,128,128]{2,1,0:T(8,128)(2,1)S(1)}, bf16[10,128,128]{2,1,0:T(8,128)(2,1)S(1)}, u32[]{:S(2)}, u32[]{:S(2)}) collective-permute-start(bf16[10,128,128]{2,1,0:T(8,128)(2,1)S(1)} %collective-permute-done.27.refs_0_), channel_id=1, source_target_pairs={{0,2},{1,3},{2,4},{3,5},{4,6},{5,7},{6,0},{7,1},{8,10},{9,11},{10,... | collective-permute-start | bytes 983048 | tf_op jit(solution)/shard_map/ppermute | solution.py:563
  34.2 0.7 copy-start.4
  34.9 0.7 copy-start.5
  37.2 22.0 %collective-permute-start.34 = (bf16[30,128,128]{2,1,0:T(8,128)(2,1)S(1)}, bf16[30,128,128]{2,1,0:T(8,128)(2,1)}, u32[]{:S(2)}, u32[]{:S(2)}) collective-permute-start(bf16[30,128,128]{2,1,0:T(8,128)(2,1)S(1)} %pack.16.refs_5_), channel_id=1, source_target_pairs={{0,16},{1,17},{2,18},{3,19},{4,20},{5,21},{6,22},{7,23},{8,24},{9,... | collective-permute-start | bytes 2949128 | tf_op jit(solution)/shard_map/ppermute | solution.py:563
  37.8 21.5 %collective-permute-start.33 = (bf16[30,128,128]{2,1,0:T(8,128)(2,1)S(1)}, bf16[30,128,128]{2,1,0:T(8,128)(2,1)S(1)}, u32[]{:S(2)}, u32[]{:S(2)}) collective-permute-start(bf16[30,128,128]{2,1,0:T(8,128)(2,1)S(1)} %pack.16.refs_5_), channel_id=1, source_target_pairs={{0,1},{1,0},{2,3},{3,2},{4,5},{5,4},{6,7},{7,6},{8,9},{9,8},{10,11... | collective-permute-start | bytes 2949128 | tf_op jit(solution)/shard_map/ppermute | solution.py:563
  38.0 13.8 %collective-permute-start.35 = (bf16[10,128,128]{2,1,0:T(8,128)(2,1)}, bf16[10,128,128]{2,1,0:T(8,128)(2,1)S(1)}, u32[]{:S(2)}, u32[]{:S(2)}) collective-permute-start(bf16[10,128,128]{2,1,0:T(8,128)(2,1)} %get-tuple-element.224.refs_8_), channel_id=1, source_target_pairs={{0,2},{1,3},{2,4},{3,5},{4,6},{5,7},{6,0},{7,1},{8,10},{9,11},{10,... | collective-permute-start | bytes 983048 | tf_op jit(solution)/shard_map/ppermute | solution.py:563
  44.0 14.0 %collective-permute-start.37 = (bf16[10,128,128]{2,1,0:T(8,128)(2,1)}, bf16[10,128,128]{2,1,0:T(8,128)(2,1)S(1)}, u32[]{:S(2)}, u32[]{:S(2)}) collective-permute-start(bf16[10,128,128]{2,1,0:T(8,128)(2,1)} %get-tuple-element.224.refs_8_), channel_id=1, source_target_pairs={{0,6},{1,7},{2,0},{3,1},{4,2},{5,3},{6,4},{7,5},{8,14},{9,15},{10,... | collective-permute-start | bytes 983048 | tf_op jit(solution)/shard_map/ppermute | solution.py:563
  51.8 7.5 %copy-start.6 = (bf16[10,128,128]{2,1,0:T(8,128)(2,1)}, bf16[10,128,128]{2,1,0:T(8,128)(2,1)S(1)}, u32[]{:S(2)}) copy-start(bf16[10,128,128]{2,1,0:T(8,128)(2,1)S(1)} %collective-permute-done.35.refs_0_) | copy-start | bytes 983044
  51.8 10.2 %collective-permute-start.36 = (bf16[10,128,128]{2,1,0:T(8,128)(2,1)S(1)}, bf16[10,128,128]{2,1,0:T(8,128)(2,1)}, u32[]{:S(2)}, u32[]{:S(2)}) collective-permute-start(bf16[10,128,128]{2,1,0:T(8,128)(2,1)S(1)} %collective-permute-done.35.refs_0_), channel_id=1, source_target_pairs={{0,2},{1,3},{2,4},{3,5},{4,6},{5,7},{6,0},{7,1},{8,10},{9,11},{10,... | collective-permute-start | bytes 983048 | tf_op jit(solution)/shard_map/ppermute | solution.py:563
  58.0 1.3 copy-start.7
  64.5 20.1 %collective-permute-start.39 = (bf16[30,128,128]{2,1,0:T(8,128)(2,1)}, bf16[30,128,128]{2,1,0:T(8,128)(2,1)}, u32[]{:S(2)}, u32[]{:S(2)}) collective-permute-start(bf16[30,128,128]{2,1,0:T(8,128)(2,1)} %pack.17.refs_9_), channel_id=1, source_target_pairs={{0,16},{1,17},{2,18},{3,19},{4,20},{5,21},{6,22},{7,23},{8,24},{9,... | collective-permute-start | bytes 2949128 | tf_op jit(solution)/shard_map/ppermute | solution.py:563
  65.9 19.6 %collective-permute-start.38 = (bf16[30,128,128]{2,1,0:T(8,128)(2,1)}, bf16[30,128,128]{2,1,0:T(8,128)(2,1)}, u32[]{:S(2)}, u32[]{:S(2)}) collective-permute-start(bf16[30,128,128]{2,1,0:T(8,128)(2,1)} %pack.17.refs_9_), channel_id=1, source_target_pairs={{0,1},{1,0},{2,3},{3,2},{4,5},{5,4},{6,7},{7,6},{8,9},{9,8},{10,11... | collective-permute-start | bytes 2949128 | tf_op jit(solution)/shard_map/ppermute | solution.py:563
  88.3 42.6 %collective-permute-start.41 = (bf16[20,128,128]{2,1,0:T(8,128)(2,1)}, bf16[20,128,128]{2,1,0:T(8,128)(2,1)}, u32[]{:S(2)}, u32[]{:S(2)}) collective-permute-start(bf16[20,128,128]{2,1,0:T(8,128)(2,1)} %get-tuple-element.230), channel_id=1, source_target_pairs={{0,1},{1,0},{2,3},{3,2},{4,5},{5,4},{6,7},{7,6},{8,9},{9,8},{10,11... | collective-permute-start | bytes 1966088 | tf_op jit(solution)/shard_map/ppermute | solution.py:563
  89.7 41.2 %collective-permute-start.40 = (bf16[20,128,128]{2,1,0:T(8,128)(2,1)}, bf16[20,128,128]{2,1,0:T(8,128)(2,1)}, u32[]{:S(2)}, u32[]{:S(2)}) collective-permute-start(bf16[20,128,128]{2,1,0:T(8,128)(2,1)} %get-tuple-element.229), channel_id=1, source_target_pairs={{0,16},{1,17},{2,18},{3,19},{4,20},{5,21},{6,22},{7,23},{8,24},{9,... | collective-permute-start | bytes 1966088 | tf_op jit(solution)/shard_map/ppermute | solution.py:563
  93.2 37.7 %collective-permute-start.42 = (bf16[20,128,128]{2,1,0:T(8,128)(2,1)}, bf16[20,128,128]{2,1,0:T(8,128)(2,1)}, u32[]{:S(2)}, u32[]{:S(2)}) collective-permute-start(bf16[20,128,128]{2,1,0:T(8,128)(2,1)} %get-tuple-element.231), channel_id=1, source_target_pairs={{0,16},{1,17},{2,18},{3,19},{4,20},{5,21},{6,22},{7,23},{8,24},{9,... | collective-permute-start | bytes 1966088 | tf_op jit(solution)/shard_map/ppermute | solution.py:563
  94.8 36.1 %copy-start.1 = (s32[32,32]{1,0:T(8,128)S(1)}, s32[32,32]{1,0:T(8,128)}, u32[]{:S(2)}) copy-start(s32[32,32]{1,0:T(8,128)} %filled.3) | copy-start | bytes 12292
  94.8 36.1 %collective-permute-start.43 = (bf16[20,128,128]{2,1,0:T(8,128)(2,1)}, bf16[20,128,128]{2,1,0:T(8,128)(2,1)}, u32[]{:S(2)}, u32[]{:S(2)}) collective-permute-start(bf16[20,128,128]{2,1,0:T(8,128)(2,1)} %get-tuple-element.232), channel_id=1, source_target_pairs={{0,1},{1,0},{2,3},{3,2},{4,5},{5,4},{6,7},{7,6},{8,9},{9,8},{10,11... | collective-permute-start | bytes 1966088 | tf_op jit(solution)/shard_map/ppermute | solution.py:563
  176.4 4.4 %collective-permute-start.44 = (f32[1024,512]{1,0:T(8,128)}, f32[1024,512]{1,0:T(8,128)S(1)}, u32[]{:S(2)}, u32[]{:S(2)}) collective-permute-start(f32[1024,512]{1,0:T(8,128)} %get-tuple-element.235), channel_id=1, source_target_pairs={{0,8},{1,9},{2,10},{3,11},{4,12},{5,13},{6,14},{7,15},{8,0},{9,1},... | collective-permute-start | bytes 6291464 | tf_op jit(solution)/shard_map/ppermute | solution.py:622
